TPU v7x, 256 devices: a whole 4x4x8 slice. The times are simulated.
256 devices in a mesh: rows: 64 (over x, z, core), grp: 4 (over y).
Axes of the slice: x: 4, y: 4, z: 8, core: 2. Of those that a mesh axis runs over, the one named last changes fastest.
Arguments:
- matrix: bfloat16 [524288, 256], P(('grp', 'rows'))
- signs: int32 [524288], P(('grp', 'rows')), may hold values from -1 to 1, as said below
- picks: int32 [16384], P(('grp', 'rows')), may hold values from 0 to 524287, as said below
Outputs:
- sketch: float32 [16384, 256], P(('grp', 'rows'))
- factor: float32 [256, 256], replicated
Inputs may be any that keep to these rules, and one draw needn't show every extreme that they name: `signs`: each entry is +1 or -1. `picks`: the indices are distinct, and the 64 indices of block b (positions b * 64 to (b + 1) * 64 - 1) lie in rows b * 2048 to (b + 1) * 2048 - 1.
All inputs are finite; a program needn't handle non-finite values.
Results may differ from a plain program's by a relative error of at most 0.0003.
Values sent between devices are 32-bit elements; how exact they have to be, the bound alone decides.
No kernel may reach another device: no remote copies, remote signals or barrier semaphores. Data moves between devices by JAX's collectives and lax.ppermute only.
A program may use at most 64 MiB of HBM per device.

v0:
```python
import math

import jax
import jax.numpy as jnp
from jax import lax
from jax.sharding import PartitionSpec as P

BLOCK = 128


def from_partner(value, axis, distance):
    return lax.ppermute(value, axis, [(i, i ^ 1 << distance) for i in range(lax.axis_size(axis))])


def sylvester(order, dtype):
    index = jnp.arange(order, dtype=jnp.int32)
    both = jnp.bitwise_and(index[:, None], index[None, :])
    parity = jnp.zeros((order, order), jnp.int32)
    for place in range(order.bit_length()):
        parity = parity + jnp.bitwise_and(jnp.right_shift(both, place), 1)
    return (1 - 2 * (parity % 2)).astype(dtype)


def combine_pair(current, partner, upper):
    return jnp.where(upper == 0, current + partner, partner - current)


def pair_rows(current):
    bits = lax.axis_size("rows").bit_length() - 1
    for place in range(bits):
        partner = from_partner(current, "rows", place)
        upper = jnp.bitwise_and(jnp.right_shift(lax.axis_index("rows"), place), 1)
        current = combine_pair(current, partner, upper)
    return current


def pair_groups(current):
    bits = lax.axis_size("grp").bit_length() - 1
    for place in range(bits):
        partner = from_partner(current, "grp", place)
        upper = jnp.bitwise_and(jnp.right_shift(lax.axis_index("grp"), place), 1)
        current = combine_pair(current, partner, upper)
    return current


def on_device(matrix, signs, picks):
    rows_dev, width = matrix.shape
    signed = matrix * signs.astype(jnp.bfloat16)[:, None]
    outer = rows_dev // BLOCK
    inner_table = sylvester(BLOCK, jnp.bfloat16)
    current = jnp.einsum(
        "ij,ojw->oiw",
        inner_table,
        signed.reshape(outer, BLOCK, width),
        preferred_element_type=jnp.float32,
    )
    outer_table = sylvester(outer, jnp.float32)
    current = jnp.einsum("po,oiw->piw", outer_table, current, precision=lax.Precision.HIGHEST)
    current = current.reshape(rows_dev, width)
    current = pair_groups(pair_rows(current))
    total_rows = rows_dev * lax.axis_size("rows") * lax.axis_size("grp")
    start = (lax.axis_index("grp") * lax.axis_size("rows") + lax.axis_index("rows")) * rows_dev
    local_picks = picks - start
    sketch = current[local_picks] / math.sqrt(total_rows)
    samples = picks.shape[0] * lax.axis_size("rows") * lax.axis_size("grp")
    partial_gram = jnp.dot(
        sketch.T, sketch, precision=lax.Precision.HIGHEST, preferred_element_type=jnp.float32
    )
    gram = lax.psum(partial_gram, ("rows", "grp")) / samples
    factor = jnp.linalg.cholesky(gram).T
    return (sketch, factor)


def solution(mesh):
    placed = (P(("grp", "rows"), None), P(("grp", "rows")), P(("grp", "rows")))
    return jax.shard_map(
        on_device,
        mesh=mesh,
        in_specs=placed,
        out_specs=(P(("grp", "rows"), None), P()),
        check_vma=False,
    )
```

profile of v0, /device:TPU:1, one launch (start us, length us, event | category | flops | bytes accessed | tf_op | source)
XLA Modules:
  0.0 767.8 jit_solution(6702671408823245494)
XLA Ops:
  7.2 0.0 all-reduce.3.cloned.1.call-start
  7.2 0.7 convert_element_type.10
  7.9 1.6 broadcast_multiply_fusion
  9.5 0.5 fusion.11
  10.0 2.1 copy.12
  12.1 3.5 fusion
  15.5 1.2 copy.8
  16.7 0.0 copy-start.2
  16.8 3.3 collective-permute-start
  20.1 3.9 collective-permute-done
  24.0 2.5 subtract_select_fusion.7
  26.5 0.1 collective-permute-start.1
  26.6 1.2 copy-done.1
  27.8 45.7 %collective-permute-done.1 = f32[2048,256]{1,0:T(8,128)} collective-permute-done((f32[2048,256]{1,0:T(8,128)S(1)}, f32[2048,256]{1,0:T(8,128)}, u32[]{:S(2)}, u32[]{:S(2)}) %collective-permute-start.1) | collective-permute-done | bytes 2097184 | tf_op jit(solution)/shard_map/ppermute | solution.py:12
  73.5 2.5 subtract_select_fusion.6
  76.0 1.7 collective-permute-start.2
  77.8 91.5 %collective-permute-done.2 = f32[2048,256]{1,0:T(8,128)} collective-permute-done((f32[2048,256]{1,0:T(8,128)S(1)}, f32[2048,256]{1,0:T(8,128)}, u32[]{:S(2)}, u32[]{:S(2)}) %collective-permute-start.2) | collective-permute-done | bytes 2097184 | tf_op jit(solution)/shard_map/ppermute | solution.py:12
  169.3 3.2 subtract_select_fusion.5
  172.5 5.0 collective-permute-start.3
  177.5 90.8 %collective-permute-done.3 = f32[2048,256]{1,0:T(8,128)} collective-permute-done((f32[2048,256]{1,0:T(8,128)}, f32[2048,256]{1,0:T(8,128)}, u32[]{:S(2)}, u32[]{:S(2)}) %collective-permute-start.3) | collective-permute-done | bytes 2097184 | tf_op jit(solution)/shard_map/ppermute | solution.py:12
  268.3 2.5 subtract_select_fusion.4
  270.8 1.1 collective-permute-start.4
  271.9 44.4 %collective-permute-done.4 = f32[2048,256]{1,0:T(8,128)} collective-permute-done((f32[2048,256]{1,0:T(8,128)S(1)}, f32[2048,256]{1,0:T(8,128)}, u32[]{:S(2)}, u32[]{:S(2)}) %collective-permute-start.4) | collective-permute-done | bytes 2097184 | tf_op jit(solution)/shard_map/ppermute | solution.py:12
  316.4 3.2 subtract_select_fusion.3
  319.6 2.6 collective-permute-start.5
  322.2 43.6 %collective-permute-done.5 = f32[2048,256]{1,0:T(8,128)} collective-permute-done((f32[2048,256]{1,0:T(8,128)}, f32[2048,256]{1,0:T(8,128)}, u32[]{:S(2)}, u32[]{:S(2)}) %collective-permute-start.5) | collective-permute-done | bytes 2097184 | tf_op jit(solution)/shard_map/ppermute | solution.py:12
  365.8 2.5 subtract_select_fusion.2
  368.3 1.4 collective-permute-start.6
  369.7 42.3 %collective-permute-done.6 = f32[2048,256]{1,0:T(8,128)} collective-permute-done((f32[2048,256]{1,0:T(8,128)S(1)}, f32[2048,256]{1,0:T(8,128)}, u32[]{:S(2)}, u32[]{:S(2)}) %collective-permute-start.6) | collective-permute-done | bytes 2097184 | tf_op jit(solution)/shard_map/ppermute | solution.py:12
  412.0 2.5 subtract_select_fusion.1
  414.5 3.3 collective-permute-start.7
  417.8 41.3 %collective-permute-done.7 = f32[2048,256]{1,0:T(8,128)} collective-permute-done((f32[2048,256]{1,0:T(8,128)S(1)}, f32[2048,256]{1,0:T(8,128)}, u32[]{:S(2)}, u32[]{:S(2)}) %collective-permute-start.7) | collective-permute-done | bytes 2097184 | tf_op jit(solution)/shard_map/ppermute | solution.py:12
  459.1 3.2 subtract_select_fusion
  462.3 2.2 gather_fusion
  464.5 0.0 copy-start.3
  464.5 1.1 fusion.48
  465.7 0.0 all-reduce.3.cloned.1.call-update
  465.7 256.6 %all-reduce.3.cloned.1.call-done = f32[256,256]{0,1:T(8,128)} async-done(((f32[256,256]{0,1:T(8,128)}), f32[256,256]{0,1:T(8,128)}) %all-reduce.3.cloned.1.call-update) | async-done | bytes 262160 | tf_op jit(solution)/shard_map/psum | solution.py:69
  722.3 1.0 broadcast_multiply_fusion.1
  723.3 0.1 copy.10
  723.4 1.0 fusion.2
  724.4 11.7 %cholesky.50 = f32[128,128]{1,0:T(8,128)S(1)} custom-call(f32[128,128]{1,0:T(8,128)S(1)} %cholesky.118), custom_call_target="Cholesky" | custom-call | tf_op jit(solution)/shard_map/jit(cholesky)/cholesky | solution.py:70
  736.2 9.8 %custom-call.11 = f32[1,128,128]{1,2,0:T(8,128)S(1)} custom-call(f32[1,128,128]{2,1,0:T(8,128)S(1)} %get-tuple-element.9), custom_call_target="InvertDiagBlocksLowerTriangular" | custom-call | tf_op jit(solution)/shard_map/jit(cholesky)/cholesky | solution.py:70
  746.0 0.2 constant_dynamic-update-slice_fusion.1
  746.2 0.3 convolution_subtract_fusion
  746.5 11.7 %cholesky.105 = f32[128,128]{1,0:T(8,128)S(1)} custom-call(f32[128,128]{1,0:T(8,128)S(1)} %convolution_subtract_fusion), custom_call_target="Cholesky" | custom-call | tf_op jit(solution)/shard_map/jit(cholesky)/cholesky | solution.py:70
  758.2 0.6 compare_reduce_fusion
  760.1 0.8 copy.11
  (15 shorter events, 0.2 us)
Async XLA Ops:
  7.2 715.1 %all-reduce.3.cloned.1.call-start = ((), (), s32[]{:S(2)}) async-start(), calls=%async_computation | async-start | bytes 524288 | tf_op jit(solution)/shard_map/psum | solution.py:69
  16.7 3.3 copy-start.2
  16.8 7.2 collective-permute-start
  26.5 1.3 copy-start.1
  26.5 47.0 %collective-permute-start.1 = (f32[2048,256]{1,0:T(8,128)S(1)}, f32[2048,256]{1,0:T(8,128)}, u32[]{:S(2)}, u32[]{:S(2)}) collective-permute-start(f32[2048,256]{1,0:T(8,128)S(1)} %subtract_select_fusion.7), channel_id=1, source_target_pairs={{0,8},{4,12},{8,0},{12,4},{16,24},{20,28},{24,16},{28,20},{32,40},... | collective-permute-start | bytes 6291464 | tf_op jit(solution)/shard_map/ppermute | solution.py:12
  76.0 93.3 %collective-permute-start.2 = (f32[2048,256]{1,0:T(8,128)S(1)}, f32[2048,256]{1,0:T(8,128)}, u32[]{:S(2)}, u32[]{:S(2)}) collective-permute-start(f32[2048,256]{1,0:T(8,128)S(1)} %subtract_select_fusion.6), channel_id=1, source_target_pairs={{0,16},{4,20},{8,24},{12,28},{16,0},{20,4},{24,8},{28,12},{32,48},... | collective-permute-start | bytes 6291464 | tf_op jit(solution)/shard_map/ppermute | solution.py:12
  172.5 95.8 %collective-permute-start.3 = (f32[2048,256]{1,0:T(8,128)}, f32[2048,256]{1,0:T(8,128)}, u32[]{:S(2)}, u32[]{:S(2)}) collective-permute-start(f32[2048,256]{1,0:T(8,128)} %subtract_select_fusion.5), channel_id=1, source_target_pairs={{0,32},{4,36},{8,40},{12,44},{16,48},{20,52},{24,56},{28,60},{32,0... | collective-permute-start | bytes 6291464 | tf_op jit(solution)/shard_map/ppermute | solution.py:12
  270.8 45.6 %collective-permute-start.4 = (f32[2048,256]{1,0:T(8,128)S(1)}, f32[2048,256]{1,0:T(8,128)}, u32[]{:S(2)}, u32[]{:S(2)}) collective-permute-start(f32[2048,256]{1,0:T(8,128)S(1)} %subtract_select_fusion.4), channel_id=1, source_target_pairs={{0,64},{4,68},{8,72},{12,76},{16,80},{20,84},{24,88},{28,92},{32,9... | collective-permute-start | bytes 6291464 | tf_op jit(solution)/shard_map/ppermute | solution.py:12
  319.6 46.3 %collective-permute-start.5 = (f32[2048,256]{1,0:T(8,128)}, f32[2048,256]{1,0:T(8,128)}, u32[]{:S(2)}, u32[]{:S(2)}) collective-permute-start(f32[2048,256]{1,0:T(8,128)} %subtract_select_fusion.3), channel_id=1, source_target_pairs={{0,128},{4,132},{8,136},{12,140},{16,144},{20,148},{24,152},{28,15... | collective-permute-start | bytes 6291464 | tf_op jit(solution)/shard_map/ppermute | solution.py:12
  368.3 1.4 copy-start
  368.3 43.7 %collective-permute-start.6 = (f32[2048,256]{1,0:T(8,128)S(1)}, f32[2048,256]{1,0:T(8,128)}, u32[]{:S(2)}, u32[]{:S(2)}) collective-permute-start(f32[2048,256]{1,0:T(8,128)S(1)} %subtract_select_fusion.2), channel_id=1, source_target_pairs={{0,1},{1,0},{2,3},{3,2},{4,5},{5,4},{6,7},{7,6},{8,9},{9,8},{10,11... | collective-permute-start | bytes 6291464 | tf_op jit(solution)/shard_map/ppermute | solution.py:12
  369.7 48.1 %copy-start.4 = (s32[64]{0:T(128)S(1)}, s32[64]{0:T(128)}, u32[]{:S(2)}) copy-start(s32[64]{0:T(128)} %param.5) | copy-start | bytes 772
  414.5 44.6 %collective-permute-start.7 = (f32[2048,256]{1,0:T(8,128)S(1)}, f32[2048,256]{1,0:T(8,128)}, u32[]{:S(2)}, u32[]{:S(2)}) collective-permute-start(f32[2048,256]{1,0:T(8,128)S(1)} %subtract_select_fusion.1), channel_id=1, source_target_pairs={{0,2},{1,3},{2,0},{3,1},{4,6},{5,7},{6,4},{7,5},{8,10},{9,11},{10,... | collective-permute-start | bytes 6291464 | tf_op jit(solution)/shard_map/ppermute | solution.py:12
  464.5 295.6 %copy-start.3 = (f32[64,256]{1,0:T(8,128)}, f32[64,256]{1,0:T(8,128)S(1)}, u32[]{:S(2)}) copy-start(f32[64,256]{1,0:T(8,128)S(1)} %broadcast_multiply_fusion.2) | copy-start | bytes 196612
Sparse Core Ops, SparseCore 0:
  465.8 256.4 all-reduce.2
where the time goes:
time: 769 us; the launch traced here: 768 us
  waiting for transfers between devices  660 us (86%)
  other arithmetic  60.2 us (8%)
  starting transfers between devices  18.6 us (2%)
  between operations  15.4 us (2%)
  local copies, waits for them, and re-layouts  7.71 us (1%)
    ppermute x8, waiting for transfers between devices, from_partner(): lax.ppermute(value, axis, [(i, i ^ 1 << distance) for i in range(lax.axis...  404 us
    psum x1, waiting for transfers between devices, on_device(): gram = lax.psum(partial_gram, ('rows', 'grp')) / samples  257 us
    another operation x6, other arithmetic, on_device(): factor = jnp.linalg.cholesky(gram).T  33.9 us
    select_n x8, other arithmetic, combine_pair(): return jnp.where(upper == 0, current + partner, partner - current)  22 us
    ppermute x8, starting transfers between devices, from_partner(): lax.ppermute(value, axis, [(i, i ^ 1 << distance) for i in range(lax.axis...  18.6 us
  transfers between devices with their start and end apart: 9, of which 9 were waited for; matrix products, arithmetic and copies ran while one was open for 0% of the time, Pallas kernels for 0%

commit v1 on v0

v1 whole, which is shorter than its diff:
```python
import math

import jax
import jax.numpy as jnp
from jax import lax
from jax.experimental import pallas as pl
from jax.experimental.pallas import tpu as pltpu
from jax.sharding import Mesh, PartitionSpec as P

NX, NZH, NZ0, NC, NY = 4, 4, 2, 2, 4
NZ = NZH * NZ0
NQ = NX * NY
ROWS = 2048
SAMP = 64
OUTER = 8
ORDER = 256
W = 256
GROUP = NC * NZ0 * NX * NY
COLS = W // GROUP
CHUNK = OUTER * 8 + 2
CHIPS = NZH * NZ0 * NX * NY
LANES = 128
F32 = jnp.float32
HIGHEST = lax.Precision.HIGHEST
VMEM = pl.BlockSpec(memory_space=pltpu.VMEM)
SMEM = pl.BlockSpec(memory_space=pltpu.SMEM)


def params(mib):
    return pltpu.CompilerParams(vmem_limit_bytes=mib * 1024 * 1024)


def shape(*sizes):
    return jax.ShapeDtypeStruct(sizes, F32)


def parity_sign(value):
    return (1 - 2 * ((value ^ (value >> 1)) & 1)).astype(F32)


def butterfly(values):
    values = list(values)
    half = 1
    while half < len(values):
        for first in range(len(values)):
            if first & half == 0:
                a, b = values[first], values[first | half]
                values[first], values[first | half] = a + b, a - b
        half *= 2
    return values


def total(parts):
    while len(parts) > 1:
        parts = [parts[k] + parts[k + 1] for k in range(0, len(parts), 2)]
    return parts[0]


def local_kernel(matrix, signs, table):
    row = lax.broadcasted_iota(jnp.int32, (ORDER, ORDER), 0)
    col = lax.broadcasted_iota(jnp.int32, (ORDER, ORDER), 1)
    both = row & col
    both = both ^ (both >> 4)
    both = both ^ (both >> 2)
    both = both ^ (both >> 1)
    hadamard = (1 - 2 * (both & 1)).astype(F32).astype(jnp.bfloat16)
    for o in range(OUTER):
        block = matrix[o * ORDER : (o + 1) * ORDER, :].astype(F32)
        sign = jnp.concatenate([signs[2 * o : 2 * o + 1, :], signs[2 * o + 1 : 2 * o + 2, :]], axis=1)
        flipped = (block.T * sign.astype(F32)).astype(jnp.bfloat16)
        table[o] = jnp.dot(flipped, hadamard, preferred_element_type=F32)


def pack_kernel(ids, table, p0, p1, p2, p3, out):
    zh = ids[0]
    sub = lax.broadcasted_iota(jnp.int32, (8, LANES), 0)
    for o in range(OUTER):
        for pair in range(GROUP // 2):
            low = table[o, pair * 8 : pair * 8 + 8, :LANES]
            high = table[o, pair * 8 : pair * 8 + 8, LANES:]
            spot = 2 * pair * CHUNK + o * 8
            out[spot : spot + 8, :] = jnp.where(sub < 4, low, pltpu.roll(high, 4, 0))
            spot += CHUNK
            out[spot : spot + 8, :] = jnp.where(sub < 4, pltpu.roll(low, 4, 0), high)
    row = lax.broadcasted_iota(jnp.int32, (2, LANES), 0)
    lane = lax.broadcasted_iota(jnp.int32, (2, LANES), 1)
    tile = jnp.zeros((2, LANES), F32)
    for d, ref in enumerate((p0, p1, p2, p3)):
        spot = zh ^ d
        value = (ref[...] & (ROWS - 1)).astype(F32)
        value = jnp.broadcast_to(jnp.concatenate([value, value], axis=1), (2, LANES))
        here = (row == (spot >> 1)) & ((lane >> 6) == (spot & 1))
        tile = jnp.where(here, value, tile)
    for k in range(GROUP):
        out[k * CHUNK + OUTER * 8 : (k + 1) * CHUNK, :] = tile


def gather_kernel(blocks, out, table):
    for high in range(32):
        values = [blocks[(high * 2 + low) * CHUNK + o * 8 : (high * 2 + low) * CHUNK + o * 8 + 8, :] for low in range(2) for o in range(OUTER)]
        for k, value in enumerate(butterfly(values)):
            table[high * 16 + k] = value
    for rest in range(16):
        values = [table[high * 16 + rest] for high in range(32)]
        for high, value in enumerate(butterfly(values)):
            table[high * 16 + rest] = value
    sub = lax.broadcasted_iota(jnp.int32, (8, LANES), 0)
    lane = lax.broadcasted_iota(jnp.int32, (8, LANES), 1)
    upper, first = sub >= 4, lane < SAMP
    for half in range(GROUP // 4):
        for zp in range(2):
            rows = []
            for c in range(NC):
                picked = []
                for ylo in range(2):
                    device = c * (GROUP // 2) + half * 2 + ylo
                    spot = device * CHUNK + OUTER * 8 + zp
                    index = blocks[spot : spot + 1, :].astype(jnp.int32)
                    index = jnp.broadcast_to(index, (8, LANES))
                    low = index & (LANES - 1)
                    level = [
                        jnp.take_along_axis(table[device * 8 + o], low, axis=1, mode="promise_in_bounds")
                        for o in range(OUTER)
                    ]
                    for place in range(3):
                        odd = (index & (ORDER << place)) != 0
                        level = [jnp.where(odd, level[k + 1], level[k]) for k in range(0, len(level), 2)]
                    same = ((index & LANES) != 0) == upper
                    picked.append(jnp.where(same, level[0], pltpu.roll(level[0], 4, 0)))
                rows.append(jnp.where(upper, picked[1], picked[0]))
            turned = [pltpu.roll(row, SAMP, 1) for row in rows]
            out[2 * zp, half * 8 : half * 8 + 8, :] = jnp.where(first, rows[0], turned[1])
            out[2 * zp + 1, half * 8 : half * 8 + 8, :] = jnp.where(first, turned[0], rows[1])


def zsum_kernel(scale, ids, blocks, out):
    zh = ids[0]
    out[...] = total([blocks[d] * (parity_sign(zh & d) * scale) for d in range(NZH)])


def gram_kernel(ids, mine, other, sketch, gram, both, turned):
    c = ids[1]
    both[pl.ds(pl.multiple_of(c * 128, 128), 128), :] = mine[...]
    both[pl.ds(pl.multiple_of((1 - c) * 128, 128), 128), :] = other[...]
    value = both[...]
    turned[...] = value.T
    sketch[...] = turned[pl.ds(pl.multiple_of(c * SAMP, SAMP), SAMP), :]
    half = both[pl.ds(pl.multiple_of(c * 128, 128), 128), :]
    gram[...] = lax.dot_general(
        half, value, (((1,), (1,)), ((), ())), precision=HIGHEST, preferred_element_type=F32
    )


def spread_kernel(scale, blocks, out):
    value = total([blocks[k] for k in range(blocks.shape[0])]) * scale
    for k in range(out.shape[0]):
        out[k] = value


def factor_kernel(gram, factor, work):
    work[...] = gram[...]
    sub = lax.broadcasted_iota(jnp.int32, (8, LANES), 0)
    lane = lax.broadcasted_iota(jnp.int32, (8, LANES), 1)
    for m in range(W // 8):
        top, at = m * 8, m * 8 % LANES
        tiles = range(m * 8 // LANES, W // LANES)
        spans = {t: slice(t * LANES, (t + 1) * LANES) for t in tiles}
        rows = [{t: jnp.broadcast_to(work[top + k : top + k + 1, spans[t]], (8, LANES)) for t in tiles} for k in range(8)]
        head = [[None] * i + [jnp.broadcast_to(rows[i][tiles[0]][:, at + j : at + j + 1], (8, LANES)) for j in range(i, 8)] for i in range(8)]
        inverse = []
        for k in range(8):
            inverse.append(lax.rsqrt(head[k][k]))
            for j in range(k + 1, 8):
                head[k][j] = head[k][j] * inverse[k]
            for t in tiles:
                rows[k][t] = rows[k][t] * inverse[k]
            for i in range(k + 1, 8):
                for j in range(i, 8):
                    head[i][j] = head[i][j] - head[k][i] * head[k][j]
                for t in tiles:
                    rows[i][t] = rows[i][t] - head[k][i] * rows[k][t]
        for t in range(W // LANES):
            if t not in spans:
                factor[top : top + 8, t * LANES : (t + 1) * LANES] = jnp.zeros((8, LANES), F32)
                continue
            value = rows[0][t]
            for k in range(1, 8):
                value = jnp.where(sub == k, rows[k][t], value)
            if t == tiles[0]:
                value = jnp.where(lane - at >= sub, value, 0.0)
            factor[top : top + 8, spans[t]] = value
        solved = [None] * 8
        for k in reversed(range(8)):
            solved[k] = {}
            for t in tiles:
                value = rows[k][t]
                for i in range(7, k, -1):
                    value = value - head[k][i] * solved[i][t]
                solved[k][t] = value * inverse[k]
        for g in range(m + 1, W // 8):
            block = work[g * 8 : g * 8 + 8, spans[tiles[0]]]
            sides = [jnp.broadcast_to(block[:, at + j : at + j + 1], (8, LANES)) for j in range(8)]
            for t in tiles:
                if m % 16 == 15 and t == tiles[0]:
                    continue
                parts = [sides[j] * solved[j][t] for j in range(8)]
                while len(parts) > 1:
                    parts = [parts[k] + parts[k + 1] for k in range(0, len(parts), 2)]
                work[g * 8 : g * 8 + 8, spans[t]] = work[g * 8 : g * 8 + 8, spans[t]] - parts[0]


def on_device(matrix, signs, picks):
    zh, c = lax.axis_index("zh"), lax.axis_index("core")
    ids = jnp.stack([zh, c]).astype(jnp.int32)
    line = [picks] + [lax.ppermute(picks, "zh", [(i, i ^ d) for i in range(NZH)]) for d in range(1, NZH)]
    line = [value.reshape(1, SAMP) for value in line]

    table = pl.pallas_call(
        local_kernel,
        out_shape=shape(OUTER, W, ORDER),
        in_specs=[VMEM, VMEM],
        out_specs=VMEM,
        compiler_params=params(16),
        name="local",
    )(matrix, signs.reshape(OUTER * 2, LANES))
    packed = pl.pallas_call(
        pack_kernel,
        out_shape=shape(GROUP * CHUNK, LANES),
        in_specs=[SMEM] + [VMEM] * 5,
        out_specs=VMEM,
        compiler_params=params(16),
        name="pack",
    )(ids, table, *line)
    packed = packed.reshape(GROUP, CHUNK // 2, 2, LANES)
    packed = lax.all_to_all(packed, ("core", "z0", "x", "y"), 0, 0, tiled=True).reshape(GROUP * CHUNK, LANES)

    sampled = pl.pallas_call(
        gather_kernel,
        out_shape=shape(NZH, CHIPS // NZH * COLS, LANES),
        in_specs=[VMEM],
        out_specs=VMEM,
        scratch_shapes=[pltpu.VMEM((GROUP * OUTER, 8, LANES), F32)],
        compiler_params=params(16),
        name="gather",
    )(packed)
    sampled = lax.all_to_all(
        sampled.reshape(CHIPS, COLS, LANES), ("zh", "z0", "x", "y"), 0, 0, tiled=True
    ).reshape(NZH, CHIPS // NZH * COLS, LANES)

    mine = pl.pallas_call(
        lambda *refs: zsum_kernel(1.0 / math.sqrt(ROWS * 256), *refs),
        out_shape=shape(128, LANES),
        in_specs=[SMEM, VMEM],
        out_specs=VMEM,
        compiler_params=params(4),
        name="zsum",
    )(ids, sampled)
    other = lax.ppermute(mine, "core", [(0, 1), (1, 0)])
    sketch, gram = pl.pallas_call(
        gram_kernel,
        out_shape=[shape(SAMP, W), shape(W // NC, W)],
        in_specs=[SMEM, VMEM, VMEM],
        out_specs=[VMEM, VMEM],
        scratch_shapes=[pltpu.VMEM((W, 128), F32), pltpu.VMEM((128, W), F32)],
        compiler_params=params(4),
        name="gram",
    )(ids, mine, other)

    def spread(blocks, count, scale, name):
        return pl.pallas_call(
            lambda *refs: spread_kernel(scale, *refs),
            out_shape=shape(count, 8, W),
            in_specs=[VMEM],
            out_specs=VMEM,
            compiler_params=params(4),
            name=name,
        )(blocks)

    gram = lax.all_to_all(gram.reshape(NQ, 8, W), ("x", "y"), 0, 0, tiled=True)
    rows = spread(gram, NZ, 1.0, "sum_xy")
    rows = lax.all_to_all(rows, ("zh", "z0"), 0, 0, tiled=True)
    rows = spread(rows, NC * NQ, 1.0 / (SAMP * 256), "sum_z")
    gram = lax.all_to_all(rows, ("core", "x", "y"), 0, 0, tiled=True).reshape(W, W)
    factor = pl.pallas_call(
        factor_kernel,
        out_shape=shape(W, W),
        in_specs=[VMEM],
        out_specs=VMEM,
        scratch_shapes=[pltpu.VMEM((W, W), F32)],
        compiler_params=params(4),
        name="factor",
    )(gram)
    return (sketch, factor)


def solution(mesh):
    devices = mesh.devices.transpose([mesh.axis_names.index(name) for name in ("rows", "grp")])
    split = Mesh(devices.reshape(NX, NZH, NZ0, NC, NY), ("x", "zh", "z0", "core", "y"))
    rows = ("y", "x", "zh", "z0", "core")
    return jax.shard_map(
        on_device,
        mesh=split,
        in_specs=(P(rows, None), P(rows), P(rows)),
        out_specs=(P(rows, None), P()),
        check_vma=False,
    )
```

time: 769 us -> 131 us (0.17)
  waiting for transfers between devices: 660 us -> 3.83 us
  blocking collectives: 0 us -> 94.9 us
  other arithmetic: 60.2 us -> 0.07 us
  Pallas kernels: 0 us -> 17.9 us
  between operations: 15.4 us -> 0.69 us
    ppermute x8 -> x4, waiting for transfers between devices: 404 us -> 3.83 us  [the longest x3 2.92 us: on_device(): lax.ppermute(picks, 'zh', [(i, i ^ d) for i in range(NZH)])]
    psum x1 -> x0, waiting for transfers between devices: 257 us -> none  [on_device(): gram = lax.psum(partial_gram, ('rows', 'grp')) / samples]
    all_to_all x0 -> x5, blocking collectives: none -> 94.9 us  [the longest x1 40.6 us: on_device(): lax.all_to_all(packed, ('core', 'z0', 'x', 'y'), 0, 0, tiled=True)]
    another operation x6 -> x1, other arithmetic: 33.9 us -> 0.07 us  [on_device(): ids = jnp.stack([zh, c]).astype(jnp.int32)]
    select_n x9 -> x0, other arithmetic: 22 us -> none  [the longest x8 22 us: combine_pair(): return jnp.where(upper == 0, current + partner, partner - current)]
    pallas_call x0 -> x8, Pallas kernels: none -> 17.9 us  [the longest x1 10.6 us: on_device(): pl.pallas_call(factor_kernel, out_shape=shape(W, W), in_specs=[VMEM], out...]
    ppermute x8 -> x4, starting transfers between devices: 18.6 us -> 11.5 us  [the longest x3 9.02 us: on_device(): lax.ppermute(picks, 'zh', [(i, i ^ d) for i in range(NZH)])]
  transfers between devices with their start and end apart: 9 -> 4, of which waited for: 9 -> 2; matrix products, arithmetic and copies ran while one was open for 0% -> 0% of each run, Pallas kernels for 0% -> 0%
where the time goes in v1:
time: 131 us
  blocking collectives  94.9 us (72%)
  Pallas kernels  17.9 us (14%)
  starting transfers between devices  11.5 us (9%)
  waiting for transfers between devices  3.83 us (3%)
  local copies, waits for them, and re-layouts  1.92 us (1%)
    all_to_all x1, blocking collectives, on_device(): lax.all_to_all(packed, ('core', 'z0', 'x', 'y'), 0, 0, tiled=True)  40.6 us
    all_to_all x1, blocking collectives, on_device(): lax.all_to_all(sampled.reshape(CHIPS, COLS, LANES), ('zh', 'z0', 'x', 'y'...  20.4 us
    all_to_all x1, blocking collectives, on_device(): lax.all_to_all(rows, ('core', 'x', 'y'), 0, 0, tiled=True).reshape(W, W)  14.9 us
    pallas_call x1, Pallas kernels, on_device(): pl.pallas_call(factor_kernel, out_shape=shape(W, W), in_specs=[VMEM], out...  10.6 us
    all_to_all x1, blocking collectives, on_device(): rows = lax.all_to_all(rows, ('zh', 'z0'), 0, 0, tiled=True)  9.6 us
    all_to_all x1, blocking collectives, on_device(): gram = lax.all_to_all(gram.reshape(NQ, 8, W), ('x', 'y'), 0, 0, tiled=True)  9.31 us
    ppermute x3, starting transfers between devices, on_device(): lax.ppermute(picks, 'zh', [(i, i ^ d) for i in range(NZH)])  9.02 us
    pallas_call x1, Pallas kernels, on_device(): pl.pallas_call(gather_kernel, out_shape=shape(NZH, CHIPS // NZH * COLS, L...  4.12 us
  transfers between devices with their start and end apart: 4, of which 2 were waited for; matrix products, arithmetic and copies ran while one was open for 0% of the time, Pallas kernels for 0%

profile of v1, /device:TPU:1, one launch (start us, length us, event | category | flops | bytes accessed | tf_op | source)
XLA Modules:
  0.0 130.8 jit_solution(18033747308514553026)
XLA Ops:
  0.6 0.0 copy-start.2
  0.6 3.9 %collective-permute-start = (s32[64]{0:T(128)}, s32[64]{0:T(128)S(1)}, u32[]{:S(2)}, u32[]{:S(2)}) collective-permute-start(s32[64]{0:T(128)} %param.5), channel_id=1, source_target_pairs={{0,16},{16,0},{32,48},{48,32},{1,17},{17,1},{33,49},{49,33},{2,18}... | collective-permute-start | bytes 776 | tf_op jit(solution)/shard_map/ppermute | solution.py:215
  4.5 4.2 %collective-permute-start.2 = (s32[64]{0:T(128)}, s32[64]{0:T(128)S(1)}, u32[]{:S(2)}, u32[]{:S(2)}) collective-permute-start(s32[64]{0:T(128)} %param.5), channel_id=1, source_target_pairs={{0,48},{16,32},{32,16},{48,0},{1,49},{17,33},{33,17},{49,1},{2,50}... | collective-permute-start | bytes 776 | tf_op jit(solution)/shard_map/ppermute | solution.py:215
  8.7 0.9 collective-permute-start.1
  9.7 0.1 pad_add_fusion.ids.refs_0_
  9.7 0.0 copy-start
  9.7 1.2 copy-done
  11.0 0.0 copy-start.1
  11.0 0.7 copy-done.1
  11.7 0.6 local.1.table
  12.2 0.0 collective-permute-done
  12.3 0.0 collective-permute-done.2
  12.3 2.9 %collective-permute-done.1 = s32[64]{0:T(128)S(1)} collective-permute-done((s32[64]{0:T(128)}, s32[64]{0:T(128)S(1)}, u32[]{:S(2)}, u32[]{:S(2)}) %collective-permute-start.1) | collective-permute-done | bytes 288 | tf_op jit(solution)/shard_map/ppermute | solution.py:215
  15.2 0.0 copy-done.2
  15.2 0.7 pack.1
  15.9 40.6 %all_to_all.25 = f32[64,33,2,128]{3,2,1,0:T(2,128)S(1)} all-to-all(f32[64,33,2,128]{3,2,1,0:T(2,128)S(1)} %bitcast.13), channel_id=1, replica_groups=mesh['x'=4,'zh'=4,'z0'=2,'core'=2,'y'=4] {'core','z0','x','y'}, dimensions={0} | all-to-all | bytes 4325376 | tf_op jit(solution)/shard_map/all_to_all | solution.py:235
  56.5 4.1 %gather.1 = f32[4,128,128]{2,1,0:T(8,128)S(1)} custom-call(f32[4224,128]{1,0:T(8,128)S(1)} %bitcast.14), custom_call_target="tpu_custom_call" | custom-call | tf_op jit(solution)/shard_map/gather/pallas_call | solution.py:237
  60.6 20.4 %all_to_all.26 = f32[128,4,128]{2,1,0:T(4,128)S(1)} all-to-all(f32[128,4,128]{2,1,0:T(4,128)S(1)} %bitcast.15), channel_id=1, replica_groups=mesh['x'=4,'zh'=4,'z0'=2,'core'=2,'y'=4] {'zh','z0','x','y'}, dimensions={0} | all-to-all | bytes 524288 | tf_op jit(solution)/shard_map/all_to_all | solution.py:246
  81.1 0.6 zsum.1.mine
  81.7 2.5 %collective-permute-start.3 = (f32[128,128]{1,0:T(8,128)S(1)}, f32[128,128]{1,0:T(8,128)S(1)}, u32[]{:S(2)}, u32[]{:S(2)}) collective-permute-start(f32[128,128]{1,0:T(8,128)S(1)} %zsum.1.mine), channel_id=1, source_target_pairs={{0,4},{4,0},{1,5},{5,1},{2,6},{6,2},{3,7},{7,3},{8,12},{12,8},{9,1... | collective-permute-start | bytes 196616 | tf_op jit(solution)/shard_map/ppermute | solution.py:258
  84.2 0.9 collective-permute-done.3.other
  85.1 1.3 %gram.1 = (f32[64,256]{1,0:T(8,128)}, f32[128,256]{1,0:T(8,128)S(1)}) custom-call(s32[2]{0:T(128)S(1)} %pad_add_fusion.ids.refs_0_, f32[128,128]{1,0:T(8,128)S(1)} %zsum.1.mine, f32[128,128]{1,0:T(8,128)S(1)} %collective-permute-done.3.other), custom_call_target="tpu_custom_call" | custom-call | tf_op jit(solution)/shard_map/gram/pallas_call | solution.py:259
  86.4 9.3 %all_to_all.27.refs_0_ = f32[16,8,256]{2,1,0:T(8,128)S(1)} all-to-all(f32[16,8,256]{2,1,0:T(8,128)S(1)} %bitcast.18), channel_id=1, replica_groups=mesh['x'=4,'zh'=4,'z0'=2,'core'=2,'y'=4] {'x','y'}, dimensions={0} | all-to-all | bytes 262144 | tf_op jit(solution)/shard_map/all_to_all | solution.py:279
  95.7 9.6 %all_to_all.28.refs_0_ = f32[8,8,256]{2,1,0:T(8,128)S(1)} all-to-all(f32[8,8,256]{2,1,0:T(8,128)S(1)} %sum_xy.1), channel_id=1, replica_groups=mesh['x'=4,'zh'=4,'z0'=2,'core'=2,'y'=4] {'zh','z0'}, dimensions={0} | all-to-all | bytes 131072 | tf_op jit(solution)/shard_map/all_to_all | solution.py:281
  105.3 14.9 %all_to_all.29 = f32[32,8,256]{2,1,0:T(8,128)S(1)} all-to-all(f32[32,8,256]{2,1,0:T(8,128)S(1)} %sum_z.1), channel_id=1, replica_groups=mesh['x'=4,'zh'=4,'z0'=2,'core'=2,'y'=4] {'core','x','y'}, dimensions={0} | all-to-all | bytes 524288 | tf_op jit(solution)/shard_map/all_to_all | solution.py:283
  120.2 10.6 %factor.1 = f32[256,256]{1,0:T(8,128)} custom-call(f32[256,256]{1,0:T(8,128)S(1)} %bitcast.17), custom_call_target="tpu_custom_call" | custom-call | tf_op jit(solution)/shard_map/factor/pallas_call | solution.py:284
  (2 shorter events, 0.0 us)
Async XLA Ops:
  0.6 14.6 %copy-start.2 = (s32[64]{0:T(128)S(1)}, s32[64]{0:T(128)}, u32[]{:S(2)}) copy-start(s32[64]{0:T(128)} %param.5) | copy-start | bytes 772
  0.6 11.6 %collective-permute-start = (s32[64]{0:T(128)}, s32[64]{0:T(128)S(1)}, u32[]{:S(2)}, u32[]{:S(2)}) collective-permute-start(s32[64]{0:T(128)} %param.5), channel_id=1, source_target_pairs={{0,16},{16,0},{32,48},{48,32},{1,17},{17,1},{33,49},{49,33},{2,18}... | collective-permute-start | bytes 776 | tf_op jit(solution)/shard_map/ppermute | solution.py:215
  4.5 7.7 %collective-permute-start.2 = (s32[64]{0:T(128)}, s32[64]{0:T(128)S(1)}, u32[]{:S(2)}, u32[]{:S(2)}) collective-permute-start(s32[64]{0:T(128)} %param.5), channel_id=1, source_target_pairs={{0,48},{16,32},{32,16},{48,0},{1,49},{17,33},{33,17},{49,1},{2,50}... | collective-permute-start | bytes 776 | tf_op jit(solution)/shard_map/ppermute | solution.py:215
  8.7 6.4 %collective-permute-start.1 = (s32[64]{0:T(128)}, s32[64]{0:T(128)S(1)}, u32[]{:S(2)}, u32[]{:S(2)}) collective-permute-start(s32[64]{0:T(128)} %param.5), channel_id=1, source_target_pairs={{0,32},{16,48},{32,0},{48,16},{1,33},{17,49},{33,1},{49,17},{2,34}... | collective-permute-start | bytes 776 | tf_op jit(solution)/shard_map/ppermute | solution.py:215
  9.7 1.2 copy-start
  11.0 0.7 copy-start.1
  81.7 3.4 %collective-permute-start.3 = (f32[128,128]{1,0:T(8,128)S(1)}, f32[128,128]{1,0:T(8,128)S(1)}, u32[]{:S(2)}, u32[]{:S(2)}) collective-permute-start(f32[128,128]{1,0:T(8,128)S(1)} %zsum.1.mine), channel_id=1, source_target_pairs={{0,4},{4,0},{1,5},{5,1},{2,6},{6,2},{3,7},{7,3},{8,12},{12,8},{9,1... | collective-permute-start | bytes 196616 | tf_op jit(solution)/shard_map/ppermute | solution.py:258

commit v2 on v1

--- a/solution.py
+++ b/solution.py
@@ -71,8 +71,7 @@
         table[o] = jnp.dot(flipped, hadamard, preferred_element_type=F32)
 
 
-def pack_kernel(ids, table, p0, p1, p2, p3, out):
-    zh = ids[0]
+def pack_kernel(table, picks, out):
     sub = lax.broadcasted_iota(jnp.int32, (8, LANES), 0)
     for o in range(OUTER):
         for pair in range(GROUP // 2):
@@ -82,40 +81,46 @@
             out[spot : spot + 8, :] = jnp.where(sub < 4, low, pltpu.roll(high, 4, 0))
             spot += CHUNK
             out[spot : spot + 8, :] = jnp.where(sub < 4, pltpu.roll(low, 4, 0), high)
-    row = lax.broadcasted_iota(jnp.int32, (2, LANES), 0)
-    lane = lax.broadcasted_iota(jnp.int32, (2, LANES), 1)
-    tile = jnp.zeros((2, LANES), F32)
-    for d, ref in enumerate((p0, p1, p2, p3)):
-        spot = zh ^ d
-        value = (ref[...] & (ROWS - 1)).astype(F32)
-        value = jnp.broadcast_to(jnp.concatenate([value, value], axis=1), (2, LANES))
-        here = (row == (spot >> 1)) & ((lane >> 6) == (spot & 1))
-        tile = jnp.where(here, value, tile)
+    value = (picks[...] & (ROWS - 1)).astype(F32)
+    value = jnp.broadcast_to(jnp.concatenate([value, value], axis=1), (2, LANES))
     for k in range(GROUP):
-        out[k * CHUNK + OUTER * 8 : (k + 1) * CHUNK, :] = tile
-
-
-def gather_kernel(blocks, out, table):
+        out[k * CHUNK + OUTER * 8 : (k + 1) * CHUNK, :] = value
+
+
+def picks_kernel(blocks, out):
+    for k in range(GROUP):
+        spot = k * CHUNK + OUTER * 8
+        out[k : k + 1, :] = blocks[spot : spot + 1, :].astype(jnp.int32)
+
+
+def transform_kernel(blocks, table):
     for high in range(32):
-        values = [blocks[(high * 2 + low) * CHUNK + o * 8 : (high * 2 + low) * CHUNK + o * 8 + 8, :] for low in range(2) for o in range(OUTER)]
+        values = [
+            blocks[(high * 2 + low) * CHUNK + o * 8 : (high * 2 + low) * CHUNK + o * 8 + 8, :]
+            for low in range(2)
+            for o in range(OUTER)
+        ]
         for k, value in enumerate(butterfly(values)):
             table[high * 16 + k] = value
     for rest in range(16):
         values = [table[high * 16 + rest] for high in range(32)]
         for high, value in enumerate(butterfly(values)):
             table[high * 16 + rest] = value
+
+
+def gather_kernel(ids, table, p0, p1, p2, p3, out):
+    zh = ids[0]
     sub = lax.broadcasted_iota(jnp.int32, (8, LANES), 0)
     lane = lax.broadcasted_iota(jnp.int32, (8, LANES), 1)
     upper, first = sub >= 4, lane < SAMP
     for half in range(GROUP // 4):
-        for zp in range(2):
+        for d, (left, right) in enumerate(((p0, p1), (p2, p3))):
             rows = []
             for c in range(NC):
                 picked = []
                 for ylo in range(2):
                     device = c * (GROUP // 2) + half * 2 + ylo
-                    spot = device * CHUNK + OUTER * 8 + zp
-                    index = blocks[spot : spot + 1, :].astype(jnp.int32)
+                    index = jnp.where(first[:1], left[device : device + 1, :], right[device : device + 1, :])
                     index = jnp.broadcast_to(index, (8, LANES))
                     low = index & (LANES - 1)
                     level = [
@@ -129,8 +134,8 @@
                     picked.append(jnp.where(same, level[0], pltpu.roll(level[0], 4, 0)))
                 rows.append(jnp.where(upper, picked[1], picked[0]))
             turned = [pltpu.roll(row, SAMP, 1) for row in rows]
-            out[2 * zp, half * 8 : half * 8 + 8, :] = jnp.where(first, rows[0], turned[1])
-            out[2 * zp + 1, half * 8 : half * 8 + 8, :] = jnp.where(first, turned[0], rows[1])
+            out[zh ^ (2 * d), half * 8 : half * 8 + 8, :] = jnp.where(first, rows[0], turned[1])
+            out[zh ^ (2 * d + 1), half * 8 : half * 8 + 8, :] = jnp.where(first, turned[0], rows[1])
 
 
 def zsum_kernel(scale, ids, blocks, out):
@@ -161,60 +166,72 @@
     work[...] = gram[...]
     sub = lax.broadcasted_iota(jnp.int32, (8, LANES), 0)
     lane = lax.broadcasted_iota(jnp.int32, (8, LANES), 1)
-    for m in range(W // 8):
-        top, at = m * 8, m * 8 % LANES
-        tiles = range(m * 8 // LANES, W // LANES)
-        spans = {t: slice(t * LANES, (t + 1) * LANES) for t in tiles}
-        rows = [{t: jnp.broadcast_to(work[top + k : top + k + 1, spans[t]], (8, LANES)) for t in tiles} for k in range(8)]
-        head = [[None] * i + [jnp.broadcast_to(rows[i][tiles[0]][:, at + j : at + j + 1], (8, LANES)) for j in range(i, 8)] for i in range(8)]
+    block = 32
+    for top in range(0, W, 8):
+        at, tile = top % LANES, top // LANES
+        spans = {t: slice(t * LANES, (t + 1) * LANES) for t in range(tile, W // LANES)}
+        rows = [
+            {t: jnp.broadcast_to(work[top + k : top + k + 1, span], (8, LANES)) for t, span in spans.items()}
+            for k in range(8)
+        ]
+        head = [
+            [None] * i + [jnp.broadcast_to(rows[i][tile][:, at + j : at + j + 1], (8, LANES)) for j in range(i, 8)]
+            for i in range(8)
+        ]
         inverse = []
         for k in range(8):
             inverse.append(lax.rsqrt(head[k][k]))
             for j in range(k + 1, 8):
                 head[k][j] = head[k][j] * inverse[k]
-            for t in tiles:
+            for t in spans:
                 rows[k][t] = rows[k][t] * inverse[k]
             for i in range(k + 1, 8):
                 for j in range(i, 8):
                     head[i][j] = head[i][j] - head[k][i] * head[k][j]
-                for t in tiles:
+                for t in spans:
                     rows[i][t] = rows[i][t] - head[k][i] * rows[k][t]
-        for t in range(W // LANES):
-            if t not in spans:
-                factor[top : top + 8, t * LANES : (t + 1) * LANES] = jnp.zeros((8, LANES), F32)
-                continue
+        for t in range(tile):
+            factor[top : top + 8, t * LANES : (t + 1) * LANES] = jnp.zeros((8, LANES), F32)
+        for t, span in spans.items():
             value = rows[0][t]
             for k in range(1, 8):
                 value = jnp.where(sub == k, rows[k][t], value)
-            if t == tiles[0]:
+            if t == tile:
                 value = jnp.where(lane - at >= sub, value, 0.0)
-            factor[top : top + 8, spans[t]] = value
-        solved = [None] * 8
-        for k in reversed(range(8)):
-            solved[k] = {}
-            for t in tiles:
-                value = rows[k][t]
-                for i in range(7, k, -1):
-                    value = value - head[k][i] * solved[i][t]
-                solved[k][t] = value * inverse[k]
-        for g in range(m + 1, W // 8):
-            block = work[g * 8 : g * 8 + 8, spans[tiles[0]]]
-            sides = [jnp.broadcast_to(block[:, at + j : at + j + 1], (8, LANES)) for j in range(8)]
-            for t in tiles:
-                if m % 16 == 15 and t == tiles[0]:
-                    continue
-                parts = [sides[j] * solved[j][t] for j in range(8)]
-                while len(parts) > 1:
-                    parts = [parts[k] + parts[k + 1] for k in range(0, len(parts), 2)]
-                work[g * 8 : g * 8 + 8, spans[t]] = work[g * 8 : g * 8 + 8, spans[t]] - parts[0]
+            factor[top : top + 8, span] = value
+        first = top // block * block
+        last = first + block
+        if top + 8 < last:
+            solved = [None] * 8
+            for k in reversed(range(8)):
+                solved[k] = {}
+                for t in spans:
+                    value = rows[k][t]
+                    for i in range(7, k, -1):
+                        value = value - head[k][i] * solved[i][t]
+                    solved[k][t] = value * inverse[k]
+            for g in range(top + 8, last, 8):
+                left = work[g : g + 8, spans[tile]]
+                sides = [jnp.broadcast_to(left[:, at + j : at + j + 1], (8, LANES)) for j in range(8)]
+                for t, span in spans.items():
+                    work[g : g + 8, span] = work[g : g + 8, span] - total([sides[j] * solved[j][t] for j in range(8)])
+        elif last < W:
+            start = last // LANES * LANES
+            done = factor[first:last, start:]
+            for a, b in ((last, last + block), (last + block, W)):
+                if a < b:
+                    work[a:b, start:] = work[a:b, start:] - lax.dot_general(
+                        done[:, a - start : b - start],
+                        done,
+                        (((0,), (0,)), ((), ())),
+                        precision=HIGHEST,
+                        preferred_element_type=F32,
+                    )
 
 
 def on_device(matrix, signs, picks):
     zh, c = lax.axis_index("zh"), lax.axis_index("core")
     ids = jnp.stack([zh, c]).astype(jnp.int32)
-    line = [picks] + [lax.ppermute(picks, "zh", [(i, i ^ d) for i in range(NZH)]) for d in range(1, NZH)]
-    line = [value.reshape(1, SAMP) for value in line]
-
     table = pl.pallas_call(
         local_kernel,
         out_shape=shape(OUTER, W, ORDER),
@@ -226,23 +243,40 @@
     packed = pl.pallas_call(
         pack_kernel,
         out_shape=shape(GROUP * CHUNK, LANES),
-        in_specs=[SMEM] + [VMEM] * 5,
+        in_specs=[VMEM] * 2,
         out_specs=VMEM,
         compiler_params=params(16),
         name="pack",
-    )(ids, table, *line)
+    )(table, picks.reshape(1, SAMP))
     packed = packed.reshape(GROUP, CHUNK // 2, 2, LANES)
     packed = lax.all_to_all(packed, ("core", "z0", "x", "y"), 0, 0, tiled=True).reshape(GROUP * CHUNK, LANES)
 
+    local = pl.pallas_call(
+        picks_kernel,
+        out_shape=jax.ShapeDtypeStruct((GROUP, LANES), jnp.int32),
+        in_specs=[VMEM],
+        out_specs=VMEM,
+        compiler_params=params(16),
+        name="picks",
+    )(packed)
+    line = [local] + [lax.ppermute(local, "zh", [(i, i ^ d) for i in range(NZH)]) for d in (1, 2, 3)]
+    table = pl.pallas_call(
+        transform_kernel,
+        out_shape=shape(GROUP * OUTER, 8, LANES),
+        in_specs=[VMEM],
+        out_specs=VMEM,
+        compiler_params=params(16),
+        cost_estimate=pl.CostEstimate(flops=10_000_000, bytes_accessed=8_000_000, transcendentals=0),
+        name="transform",
+    )(packed)
     sampled = pl.pallas_call(
         gather_kernel,
         out_shape=shape(NZH, CHIPS // NZH * COLS, LANES),
-        in_specs=[VMEM],
-        out_specs=VMEM,
-        scratch_shapes=[pltpu.VMEM((GROUP * OUTER, 8, LANES), F32)],
+        in_specs=[SMEM] + [VMEM] * 5,
+        out_specs=VMEM,
         compiler_params=params(16),
         name="gather",
-    )(packed)
+    )(ids, table, *line)
     sampled = lax.all_to_all(
         sampled.reshape(CHIPS, COLS, LANES), ("zh", "z0", "x", "y"), 0, 0, tiled=True
     ).reshape(NZH, CHIPS // NZH * COLS, LANES)

time: 131 us -> 131 us (level)
  blocking collectives: 94.9 us -> 54.1 us
  waiting for transfers between devices: 3.83 us -> 34.9 us
  starting transfers between devices: 11.5 us -> 21.6 us
  Pallas kernels: 17.9 us -> 15.9 us
  local copies, waits for them, and re-layouts: 1.92 us -> 3.28 us
    all_to_all x1 -> x0, blocking collectives: 40.6 us -> none  [on_device(): lax.all_to_all(packed, ('core', 'z0', 'x', 'y'), 0, 0, tiled=True)]
    all_to_all x0 -> x1, waiting for transfers between devices: none -> 29.2 us  [on_device(): lax.all_to_all(packed, ('core', 'z0', 'x', 'y'), 0, 0, tiled=True)]
    all_to_all x0 -> x1, starting transfers between devices: none -> 10.4 us  [on_device(): lax.all_to_all(packed, ('core', 'z0', 'x', 'y'), 0, 0, tiled=True)]
    pallas_call x1, Pallas kernels: 10.6 us -> 8.49 us  [on_device(): pl.pallas_call(factor_kernel, out_shape=shape(W, W), in_specs=[VMEM], out...]
    ppermute x3, waiting for transfers between devices: 2.92 us -> 4.81 us  [on_device(): lax.ppermute(local, 'zh', [(i, i ^ d) for i in range(NZH)])]
    ppermute x3, starting transfers between devices: 9.02 us -> 7.4 us  [on_device(): lax.ppermute(local, 'zh', [(i, i ^ d) for i in range(NZH)])]
    unnamed x6 -> x8, local copies, waits for them, and re-layouts: 1.92 us -> 3.28 us
  transfers between devices with their start and end apart: 4 -> 5, of which waited for: 2 -> 3; matrix products, arithmetic and copies ran while one was open for 0% -> 0% of each run, Pallas kernels for 0% -> 1%
where the time goes in v2:
time: 131 us
  blocking collectives  54.1 us (41%)
  waiting for transfers between devices  34.9 us (27%)
  starting transfers between devices  21.6 us (16%)
  Pallas kernels  15.9 us (12%)
  local copies, waits for them, and re-layouts  3.28 us (3%)
    all_to_all x1, waiting for transfers between devices, on_device(): lax.all_to_all(packed, ('core', 'z0', 'x', 'y'), 0, 0, tiled=True)  29.2 us
    all_to_all x1, blocking collectives, on_device(): lax.all_to_all(sampled.reshape(CHIPS, COLS, LANES), ('zh', 'z0', 'x', 'y'...  20.3 us
    all_to_all x1, blocking collectives, on_device(): lax.all_to_all(rows, ('core', 'x', 'y'), 0, 0, tiled=True).reshape(W, W)  14.9 us
    all_to_all x1, starting transfers between devices, on_device(): lax.all_to_all(packed, ('core', 'z0', 'x', 'y'), 0, 0, tiled=True)  10.4 us
    all_to_all x1, blocking collectives, on_device(): rows = lax.all_to_all(rows, ('zh', 'z0'), 0, 0, tiled=True)  9.6 us
    all_to_all x1, blocking collectives, on_device(): gram = lax.all_to_all(gram.reshape(NQ, 8, W), ('x', 'y'), 0, 0, tiled=True)  9.31 us
    pallas_call x1, Pallas kernels, on_device(): pl.pallas_call(factor_kernel, out_shape=shape(W, W), in_specs=[VMEM], out...  8.49 us
    ppermute x3, starting transfers between devices, on_device(): lax.ppermute(local, 'zh', [(i, i ^ d) for i in range(NZH)])  7.4 us
  transfers between devices with their start and end apart: 5, of which 3 were waited for; matrix products, arithmetic and copies ran while one was open for 0% of the time, Pallas kernels for 1%

profile of v2, /device:TPU:1, one launch (start us, length us, event | category | flops | bytes accessed | tf_op | source)
XLA Modules:
  0.0 130.5 jit_solution(4669641579048956973)
XLA Ops:
  0.6 0.0 copy-start.3
  0.6 0.0 copy-start.1
  0.6 1.2 copy-done.1
  1.9 0.0 copy-start.2
  1.9 0.7 copy-done.2
  2.6 0.6 local.1.table
  3.2 0.0 copy-done.3
  3.2 0.2 pack.1
  3.4 0.0 copy-start
  3.4 1.3 %copy-done = f32[4224,128]{1,0:T(8,128)} copy-done((f32[4224,128]{1,0:T(8,128)}, f32[4224,128]{1,0:T(8,128)S(1)}, u32[]{:S(2)}) %copy-start) | copy-done | bytes 2162712
  4.8 10.4 %all-to-all-start = ((f32[64,33,2,128]{3,2,1,0:T(2,128)}), f32[64,33,2,128]{3,2,1,0:T(2,128)S(1)}, u32[]{:S(2)}, u32[]{:S(2)}) async-start(f32[64,33,2,128]{3,2,1,0:T(2,128)} %bitcast.12), calls=%async_computation | async-start | bytes 4325376 | tf_op jit(solution)/shard_map/all_to_all | solution.py:252
  15.2 29.2 %all-to-all-done = f32[64,33,2,128]{3,2,1,0:T(2,128)S(1)} async-done(((f32[64,33,2,128]{3,2,1,0:T(2,128)}), f32[64,33,2,128]{3,2,1,0:T(2,128)S(1)}, u32[]{:S(2)}, u32[]{:S(2)}) %all-to-all-start) | async-done | bytes 2162720 | tf_op jit(solution)/shard_map/all_to_all | solution.py:252
  44.4 5.2 %collective-permute-start.2 = (s32[64,128]{1,0:T(8,128)S(1)}, s32[64,128]{1,0:T(8,128)S(1)}, u32[]{:S(2)}, u32[]{:S(2)}) collective-permute-start(s32[64,128]{1,0:T(8,128)S(1)} %picks.1.p0), channel_id=1, source_target_pairs={{0,48},{16,32},{32,16},{48,0},{1,49},{17,33},{33,17},{49,1},{2,50}... | collective-permute-start | bytes 98312 | tf_op jit(solution)/shard_map/ppermute | solution.py:262
  49.7 1.2 collective-permute-start.1
  50.8 1.0 collective-permute-start
  51.8 0.1 pad_add_fusion.ids.refs_0_
  51.9 0.8 transform.1.table
  52.7 0.0 collective-permute-done.2.p3
  52.7 4.8 %collective-permute-done.1.p2 = s32[64,128]{1,0:T(8,128)S(1)} collective-permute-done((s32[64,128]{1,0:T(8,128)S(1)}, s32[64,128]{1,0:T(8,128)S(1)}, u32[]{:S(2)}, u32[]{:S(2)}) %collective-permute-start.1) | collective-permute-done | bytes 32800 | tf_op jit(solution)/shard_map/ppermute | solution.py:262
  57.5 0.0 collective-permute-done.p1
  57.5 3.9 %gather.1 = f32[4,128,128]{2,1,0:T(8,128)S(1)} custom-call(s32[2]{0:T(128)S(1)} %pad_add_fusion.ids.refs_0_, f32[512,8,128]{2,1,0:T(8,128)S(1)} %transform.1.table, s32[64,128]{1,0:T(8,128)S(1)} %picks.1.p0, s32[64,128]{1,0:T(8,128)S(1)} %collective-permute-done.p1, s32[64,128]{1,0:T(8,128)S(1)} %collective-permute-done.1.p2, ...), custom_call_target="tpu_custom_call" | custom-call | tf_op jit(solution)/shard_map/gather/pallas_call | solution.py:272
  61.4 20.3 %all_to_all.25 = f32[128,4,128]{2,1,0:T(4,128)S(1)} all-to-all(f32[128,4,128]{2,1,0:T(4,128)S(1)} %bitcast.15), channel_id=1, replica_groups=mesh['x'=4,'zh'=4,'z0'=2,'core'=2,'y'=4] {'zh','z0','x','y'}, dimensions={0} | all-to-all | bytes 524288 | tf_op jit(solution)/shard_map/all_to_all | solution.py:280
  81.7 0.6 zsum.1.mine
  82.3 3.7 %collective-permute-start.3 = (f32[128,128]{1,0:T(8,128)S(1)}, f32[128,128]{1,0:T(8,128)S(1)}, u32[]{:S(2)}, u32[]{:S(2)}) collective-permute-start(f32[128,128]{1,0:T(8,128)S(1)} %zsum.1.mine), channel_id=1, source_target_pairs={{0,4},{4,0},{1,5},{5,1},{2,6},{6,2},{3,7},{7,3},{8,12},{12,8},{9,1... | collective-permute-start | bytes 196616 | tf_op jit(solution)/shard_map/ppermute | solution.py:292
  86.0 0.9 collective-permute-done.3.other
  86.9 1.3 %gram.1 = (f32[64,256]{1,0:T(8,128)}, f32[128,256]{1,0:T(8,128)S(1)}) custom-call(s32[2]{0:T(128)S(1)} %pad_add_fusion.ids.refs_0_, f32[128,128]{1,0:T(8,128)S(1)} %zsum.1.mine, f32[128,128]{1,0:T(8,128)S(1)} %collective-permute-done.3.other), custom_call_target="tpu_custom_call" | custom-call | tf_op jit(solution)/shard_map/gram/pallas_call | solution.py:293
  88.2 9.3 %all_to_all.26.refs_0_ = f32[16,8,256]{2,1,0:T(8,128)S(1)} all-to-all(f32[16,8,256]{2,1,0:T(8,128)S(1)} %bitcast.16), channel_id=1, replica_groups=mesh['x'=4,'zh'=4,'z0'=2,'core'=2,'y'=4] {'x','y'}, dimensions={0} | all-to-all | bytes 262144 | tf_op jit(solution)/shard_map/all_to_all | solution.py:313
  97.5 9.6 %all_to_all.27.refs_0_ = f32[8,8,256]{2,1,0:T(8,128)S(1)} all-to-all(f32[8,8,256]{2,1,0:T(8,128)S(1)} %sum_xy.1), channel_id=1, replica_groups=mesh['x'=4,'zh'=4,'z0'=2,'core'=2,'y'=4] {'zh','z0'}, dimensions={0} | all-to-all | bytes 131072 | tf_op jit(solution)/shard_map/all_to_all | solution.py:315
  107.2 14.9 %all_to_all.28 = f32[32,8,256]{2,1,0:T(8,128)S(1)} all-to-all(f32[32,8,256]{2,1,0:T(8,128)S(1)} %sum_z.1), channel_id=1, replica_groups=mesh['x'=4,'zh'=4,'z0'=2,'core'=2,'y'=4] {'core','x','y'}, dimensions={0} | all-to-all | bytes 524288 | tf_op jit(solution)/shard_map/all_to_all | solution.py:317
  122.1 8.5 %factor.1 = f32[256,256]{1,0:T(8,128)} custom-call(f32[256,256]{1,0:T(8,128)S(1)} %bitcast.14), custom_call_target="tpu_custom_call" | custom-call | tf_op jit(solution)/shard_map/factor/pallas_call | solution.py:318
  (3 shorter events, 0.1 us)
Async XLA Ops:
  0.6 2.5 %copy-start.3 = (s32[64]{0:T(128)S(1)}, s32[64]{0:T(128)}, u32[]{:S(2)}) copy-start(s32[64]{0:T(128)} %param.5) | copy-start | bytes 772
  0.6 1.2 copy-start.1
  1.9 0.7 copy-start.2
  3.4 1.4 %copy-start = (f32[4224,128]{1,0:T(8,128)}, f32[4224,128]{1,0:T(8,128)S(1)}, u32[]{:S(2)}) copy-start(f32[4224,128]{1,0:T(8,128)S(1)} %pack.1) | copy-start | bytes 6488068
  4.8 39.6 %all-to-all-start = ((f32[64,33,2,128]{3,2,1,0:T(2,128)}), f32[64,33,2,128]{3,2,1,0:T(2,128)S(1)}, u32[]{:S(2)}, u32[]{:S(2)}) async-start(f32[64,33,2,128]{3,2,1,0:T(2,128)} %bitcast.12), calls=%async_computation | async-start | bytes 4325376 | tf_op jit(solution)/shard_map/all_to_all | solution.py:252
  44.4 8.3 %collective-permute-start.2 = (s32[64,128]{1,0:T(8,128)S(1)}, s32[64,128]{1,0:T(8,128)S(1)}, u32[]{:S(2)}, u32[]{:S(2)}) collective-permute-start(s32[64,128]{1,0:T(8,128)S(1)} %picks.1.p0), channel_id=1, source_target_pairs={{0,48},{16,32},{32,16},{48,0},{1,49},{17,33},{33,17},{49,1},{2,50}... | collective-permute-start | bytes 98312 | tf_op jit(solution)/shard_map/ppermute | solution.py:262
  49.7 7.9 %collective-permute-start.1 = (s32[64,128]{1,0:T(8,128)S(1)}, s32[64,128]{1,0:T(8,128)S(1)}, u32[]{:S(2)}, u32[]{:S(2)}) collective-permute-start(s32[64,128]{1,0:T(8,128)S(1)} %picks.1.p0), channel_id=1, source_target_pairs={{0,32},{16,48},{32,0},{48,16},{1,33},{17,49},{33,1},{49,17},{2,34}... | collective-permute-start | bytes 98312 | tf_op jit(solution)/shard_map/ppermute | solution.py:262
  50.8 6.7 %collective-permute-start = (s32[64,128]{1,0:T(8,128)S(1)}, s32[64,128]{1,0:T(8,128)S(1)}, u32[]{:S(2)}, u32[]{:S(2)}) collective-permute-start(s32[64,128]{1,0:T(8,128)S(1)} %picks.1.p0), channel_id=1, source_target_pairs={{0,16},{16,0},{32,48},{48,32},{1,17},{17,1},{33,49},{49,33},{2,18}... | collective-permute-start | bytes 98312 | tf_op jit(solution)/shard_map/ppermute | solution.py:262
  82.3 4.6 %collective-permute-start.3 = (f32[128,128]{1,0:T(8,128)S(1)}, f32[128,128]{1,0:T(8,128)S(1)}, u32[]{:S(2)}, u32[]{:S(2)}) collective-permute-start(f32[128,128]{1,0:T(8,128)S(1)} %zsum.1.mine), channel_id=1, source_target_pairs={{0,4},{4,0},{1,5},{5,1},{2,6},{6,2},{3,7},{7,3},{8,12},{12,8},{9,1... | collective-permute-start | bytes 196616 | tf_op jit(solution)/shard_map/ppermute | solution.py:292

commit v3 on v2

--- a/solution.py
+++ b/solution.py
@@ -71,7 +71,7 @@
         table[o] = jnp.dot(flipped, hadamard, preferred_element_type=F32)
 
 
-def pack_kernel(table, picks, out):
+def pack_kernel(ids, table, p0, p1, p2, p3, out):
     sub = lax.broadcasted_iota(jnp.int32, (8, LANES), 0)
     for o in range(OUTER):
         for pair in range(GROUP // 2):
@@ -81,46 +81,42 @@
             out[spot : spot + 8, :] = jnp.where(sub < 4, low, pltpu.roll(high, 4, 0))
             spot += CHUNK
             out[spot : spot + 8, :] = jnp.where(sub < 4, pltpu.roll(low, 4, 0), high)
-    value = (picks[...] & (ROWS - 1)).astype(F32)
-    value = jnp.broadcast_to(jnp.concatenate([value, value], axis=1), (2, LANES))
+    zh = ids[0]
+    row = lax.broadcasted_iota(jnp.int32, (2, LANES), 0)
+    lane = lax.broadcasted_iota(jnp.int32, (2, LANES), 1)
+    tile = jnp.zeros((2, LANES), F32)
+    for d, ref in enumerate((p0, p1, p2, p3)):
+        place = zh ^ d
+        value = (ref[...] & (ROWS - 1)).astype(F32)
+        value = jnp.broadcast_to(jnp.concatenate([value, value], axis=1), (2, LANES))
+        here = (row == (place >> 1)) & ((lane >> 6) == (place & 1))
+        tile = jnp.where(here, value, tile)
     for k in range(GROUP):
-        out[k * CHUNK + OUTER * 8 : (k + 1) * CHUNK, :] = value
-
-
-def picks_kernel(blocks, out):
-    for k in range(GROUP):
-        spot = k * CHUNK + OUTER * 8
-        out[k : k + 1, :] = blocks[spot : spot + 1, :].astype(jnp.int32)
-
-
-def transform_kernel(blocks, table):
+        out[k * CHUNK + OUTER * 8 : (k + 1) * CHUNK, :] = tile
+
+
+def gather_kernel(blocks, out, table):
     for high in range(32):
-        values = [
-            blocks[(high * 2 + low) * CHUNK + o * 8 : (high * 2 + low) * CHUNK + o * 8 + 8, :]
-            for low in range(2)
-            for o in range(OUTER)
-        ]
+        values = [blocks[(high * 2 + low) * CHUNK + o * 8 : (high * 2 + low) * CHUNK + o * 8 + 8, :] for low in range(2) for o in range(OUTER)]
         for k, value in enumerate(butterfly(values)):
             table[high * 16 + k] = value
     for rest in range(16):
         values = [table[high * 16 + rest] for high in range(32)]
         for high, value in enumerate(butterfly(values)):
             table[high * 16 + rest] = value
-
-
-def gather_kernel(ids, table, p0, p1, p2, p3, out):
-    zh = ids[0]
     sub = lax.broadcasted_iota(jnp.int32, (8, LANES), 0)
     lane = lax.broadcasted_iota(jnp.int32, (8, LANES), 1)
     upper, first = sub >= 4, lane < SAMP
     for half in range(GROUP // 4):
-        for d, (left, right) in enumerate(((p0, p1), (p2, p3))):
+        z0, spot = half // (NQ // 2), half % (NQ // 2) * 8
+        for zp in range(2):
             rows = []
             for c in range(NC):
                 picked = []
                 for ylo in range(2):
-                    device = c * (GROUP // 2) + half * 2 + ylo
-                    index = jnp.where(first[:1], left[device : device + 1, :], right[device : device + 1, :])
+                    device = (z0 * NC + c) * NQ + spot // 4 + ylo
+                    row = device * CHUNK + OUTER * 8 + zp
+                    index = blocks[row : row + 1, :].astype(jnp.int32)
                     index = jnp.broadcast_to(index, (8, LANES))
                     low = index & (LANES - 1)
                     level = [
@@ -134,19 +130,24 @@
                     picked.append(jnp.where(same, level[0], pltpu.roll(level[0], 4, 0)))
                 rows.append(jnp.where(upper, picked[1], picked[0]))
             turned = [pltpu.roll(row, SAMP, 1) for row in rows]
-            out[zh ^ (2 * d), half * 8 : half * 8 + 8, :] = jnp.where(first, rows[0], turned[1])
-            out[zh ^ (2 * d + 1), half * 8 : half * 8 + 8, :] = jnp.where(first, turned[0], rows[1])
+            out[z0, 2 * zp, spot : spot + 8, :] = jnp.where(first, rows[0], turned[1])
+            out[z0, 2 * zp + 1, spot : spot + 8, :] = jnp.where(first, turned[0], rows[1])
 
 
 def zsum_kernel(scale, ids, blocks, out):
     zh = ids[0]
-    out[...] = total([blocks[d] * (parity_sign(zh & d) * scale) for d in range(NZH)])
+    for z0 in range(NZ0):
+        parts = [blocks[z0, d] * (parity_sign(zh & d) * scale) for d in range(NZH)]
+        out[z0 * NQ * COLS : (z0 + 1) * NQ * COLS, :] = total(parts)
 
 
 def gram_kernel(ids, mine, other, sketch, gram, both, turned):
     c = ids[1]
-    both[pl.ds(pl.multiple_of(c * 128, 128), 128), :] = mine[...]
-    both[pl.ds(pl.multiple_of((1 - c) * 128, 128), 128), :] = other[...]
+    part = NQ * COLS
+    for z0 in range(NZ0):
+        rows = slice(z0 * part, (z0 + 1) * part)
+        both[pl.ds(pl.multiple_of((z0 * NC + c) * part, part), part), :] = mine[rows, :]
+        both[pl.ds(pl.multiple_of((z0 * NC + 1 - c) * part, part), part), :] = other[rows, :]
     value = both[...]
     turned[...] = value.T
     sketch[...] = turned[pl.ds(pl.multiple_of(c * SAMP, SAMP), SAMP), :]
@@ -232,6 +233,10 @@
 def on_device(matrix, signs, picks):
     zh, c = lax.axis_index("zh"), lax.axis_index("core")
     ids = jnp.stack([zh, c]).astype(jnp.int32)
+    matrix, ids = lax.optimization_barrier((matrix, ids))
+    line = [picks] + [lax.ppermute(picks, "zh", [(i, i ^ d) for i in range(NZH)]) for d in range(1, NZH)]
+    line = [value.reshape(1, SAMP) for value in line]
+
     table = pl.pallas_call(
         local_kernel,
         out_shape=shape(OUTER, W, ORDER),
@@ -243,43 +248,26 @@
     packed = pl.pallas_call(
         pack_kernel,
         out_shape=shape(GROUP * CHUNK, LANES),
-        in_specs=[VMEM] * 2,
+        in_specs=[SMEM] + [VMEM] * 5,
         out_specs=VMEM,
         compiler_params=params(16),
         name="pack",
-    )(table, picks.reshape(1, SAMP))
+    )(ids, table, *line)
     packed = packed.reshape(GROUP, CHUNK // 2, 2, LANES)
-    packed = lax.all_to_all(packed, ("core", "z0", "x", "y"), 0, 0, tiled=True).reshape(GROUP * CHUNK, LANES)
-
-    local = pl.pallas_call(
-        picks_kernel,
-        out_shape=jax.ShapeDtypeStruct((GROUP, LANES), jnp.int32),
-        in_specs=[VMEM],
-        out_specs=VMEM,
-        compiler_params=params(16),
-        name="picks",
-    )(packed)
-    line = [local] + [lax.ppermute(local, "zh", [(i, i ^ d) for i in range(NZH)]) for d in (1, 2, 3)]
-    table = pl.pallas_call(
-        transform_kernel,
-        out_shape=shape(GROUP * OUTER, 8, LANES),
-        in_specs=[VMEM],
-        out_specs=VMEM,
-        compiler_params=params(16),
-        cost_estimate=pl.CostEstimate(flops=10_000_000, bytes_accessed=8_000_000, transcendentals=0),
-        name="transform",
-    )(packed)
+    packed = lax.all_to_all(packed, ("z0", "core", "x", "y"), 0, 0, tiled=True).reshape(GROUP * CHUNK, LANES)
+
     sampled = pl.pallas_call(
         gather_kernel,
-        out_shape=shape(NZH, CHIPS // NZH * COLS, LANES),
-        in_specs=[SMEM] + [VMEM] * 5,
-        out_specs=VMEM,
+        out_shape=shape(NZ0, NZH, NQ * COLS, LANES),
+        in_specs=[VMEM],
+        out_specs=VMEM,
+        scratch_shapes=[pltpu.VMEM((GROUP * OUTER, 8, LANES), F32)],
         compiler_params=params(16),
         name="gather",
-    )(ids, table, *line)
+    )(packed)
     sampled = lax.all_to_all(
-        sampled.reshape(CHIPS, COLS, LANES), ("zh", "z0", "x", "y"), 0, 0, tiled=True
-    ).reshape(NZH, CHIPS // NZH * COLS, LANES)
+        sampled.reshape(CHIPS, COLS, LANES), ("z0", "zh", "x", "y"), 0, 0, tiled=True
+    ).reshape(NZ0, NZH, NQ * COLS, LANES)
 
     mine = pl.pallas_call(
         lambda *refs: zsum_kernel(1.0 / math.sqrt(ROWS * 256), *refs),

time: 131 us -> 128 us (0.977)
  blocking collectives: 54.1 us -> 92.8 us
  waiting for transfers between devices: 34.9 us -> 3.83 us
  starting transfers between devices: 21.6 us -> 12.4 us
  local copies, waits for them, and re-layouts: 3.28 us -> 1.92 us
    all_to_all x1 -> x2, blocking collectives: 20.3 us -> 57.3 us  [the longest x1 40.5 us: on_device(): lax.all_to_all(packed, ('z0', 'core', 'x', 'y'), 0, 0, tiled=True)]
    all_to_all x1 -> x0, waiting for transfers between devices: 29.2 us -> none  [on_device(): lax.all_to_all(packed, ('core', 'z0', 'x', 'y'), 0, 0, tiled=True)]
    all_to_all x1 -> x0, starting transfers between devices: 10.4 us -> none  [on_device(): lax.all_to_all(packed, ('core', 'z0', 'x', 'y'), 0, 0, tiled=True)]
    ppermute x3, waiting for transfers between devices: 4.81 us -> 2.92 us  [on_device(): lax.ppermute(picks, 'zh', [(i, i ^ d) for i in range(NZH)])]
    ppermute x3, starting transfers between devices: 7.4 us -> 9.02 us  [on_device(): lax.ppermute(picks, 'zh', [(i, i ^ d) for i in range(NZH)])]
    unnamed x8 -> x6, local copies, waits for them, and re-layouts: 3.28 us -> 1.92 us
    pallas_call x3 -> x1, Pallas kernels: 4.7 us -> 4.14 us  [on_device(): pl.pallas_call(gather_kernel, out_shape=shape(NZ0, NZH, NQ * COLS, LANES)...]
  transfers between devices with their start and end apart: 5 -> 4, of which waited for: 3 -> 2; matrix products, arithmetic and copies ran while one was open for 0% -> 0% of each run, Pallas kernels for 1% -> 0%
where the time goes in v3:
time: 128 us; the launch traced here: 127 us
  blocking collectives  92.8 us (72%)
  Pallas kernels  15.8 us (12%)
  starting transfers between devices  12.4 us (10%)
  waiting for transfers between devices  3.83 us (3%)
  local copies, waits for them, and re-layouts  1.92 us (2%)
    all_to_all x1, blocking collectives, on_device(): lax.all_to_all(packed, ('z0', 'core', 'x', 'y'), 0, 0, tiled=True)  40.5 us
    all_to_all x1, blocking collectives, on_device(): lax.all_to_all(sampled.reshape(CHIPS, COLS, LANES), ('z0', 'zh', 'x', 'y'...  16.8 us
    all_to_all x1, blocking collectives, on_device(): lax.all_to_all(rows, ('core', 'x', 'y'), 0, 0, tiled=True).reshape(W, W)  15.2 us
    all_to_all x1, blocking collectives, on_device(): gram = lax.all_to_all(gram.reshape(NQ, 8, W), ('x', 'y'), 0, 0, tiled=True)  10.5 us
    all_to_all x1, blocking collectives, on_device(): rows = lax.all_to_all(rows, ('zh', 'z0'), 0, 0, tiled=True)  9.71 us
    ppermute x3, starting transfers between devices, on_device(): lax.ppermute(picks, 'zh', [(i, i ^ d) for i in range(NZH)])  9.02 us
    pallas_call x1, Pallas kernels, on_device(): pl.pallas_call(factor_kernel, out_shape=shape(W, W), in_specs=[VMEM], out...  8.49 us
    pallas_call x1, Pallas kernels, on_device(): pl.pallas_call(gather_kernel, out_shape=shape(NZ0, NZH, NQ * COLS, LANES)...  4.14 us
  transfers between devices with their start and end apart: 4, of which 2 were waited for; matrix products, arithmetic and copies ran while one was open for 0% of the time, Pallas kernels for 0%

profile of v3, /device:TPU:1, one launch (start us, length us, event | category | flops | bytes accessed | tf_op | source)
XLA Modules:
  0.0 127.5 jit_solution(18323405582075174740)
XLA Ops:
  0.6 0.0 copy-start.2
  0.6 3.9 %collective-permute-start = (s32[64]{0:T(128)}, s32[64]{0:T(128)S(1)}, u32[]{:S(2)}, u32[]{:S(2)}) collective-permute-start(s32[64]{0:T(128)} %param.5), channel_id=1, source_target_pairs={{0,16},{16,0},{32,48},{48,32},{1,17},{17,1},{33,49},{49,33},{2,18}... | collective-permute-start | bytes 776 | tf_op jit(solution)/shard_map/ppermute | solution.py:237
  4.5 4.2 %collective-permute-start.2 = (s32[64]{0:T(128)}, s32[64]{0:T(128)S(1)}, u32[]{:S(2)}, u32[]{:S(2)}) collective-permute-start(s32[64]{0:T(128)} %param.5), channel_id=1, source_target_pairs={{0,48},{16,32},{32,16},{48,0},{1,49},{17,33},{33,17},{49,1},{2,50}... | collective-permute-start | bytes 776 | tf_op jit(solution)/shard_map/ppermute | solution.py:237
  8.7 0.9 collective-permute-start.1
  9.7 0.1 pad_add_fusion.ids.refs_0_
  9.7 0.0 copy-start
  9.7 1.2 copy-done
  11.0 0.0 copy-start.1
  11.0 0.7 copy-done.1
  11.7 0.6 local.1.table
  12.2 0.0 collective-permute-done
  12.3 0.0 collective-permute-done.2
  12.3 2.9 %collective-permute-done.1 = s32[64]{0:T(128)S(1)} collective-permute-done((s32[64]{0:T(128)}, s32[64]{0:T(128)S(1)}, u32[]{:S(2)}, u32[]{:S(2)}) %collective-permute-start.1) | collective-permute-done | bytes 288 | tf_op jit(solution)/shard_map/ppermute | solution.py:237
  15.2 0.0 copy-done.2
  15.2 0.7 pack.1
  15.9 40.5 %all_to_all.25 = f32[64,33,2,128]{3,2,1,0:T(2,128)S(1)} all-to-all(f32[64,33,2,128]{3,2,1,0:T(2,128)S(1)} %bitcast.13), channel_id=1, replica_groups=mesh['x'=4,'zh'=4,'z0'=2,'core'=2,'y'=4] {'z0','core','x','y'}, dimensions={0} | all-to-all | bytes 4325376 | tf_op jit(solution)/shard_map/all_to_all | solution.py:257
  56.4 4.1 %gather.1 = f32[2,4,64,128]{3,2,1,0:T(8,128)S(1)} custom-call(f32[4224,128]{1,0:T(8,128)S(1)} %bitcast.14), custom_call_target="tpu_custom_call" | custom-call | tf_op jit(solution)/shard_map/gather/pallas_call | solution.py:259
  60.6 16.8 %all_to_all.26 = f32[128,4,128]{2,1,0:T(4,128)S(1)} all-to-all(f32[128,4,128]{2,1,0:T(4,128)S(1)} %bitcast.15), channel_id=1, replica_groups=mesh['x'=4,'zh'=4,'z0'=2,'core'=2,'y'=4] {'z0','zh','x','y'}, dimensions={0} | all-to-all | bytes 524288 | tf_op jit(solution)/shard_map/all_to_all | solution.py:268
  77.4 0.6 zsum.1.mine
  78.0 3.3 %collective-permute-start.3 = (f32[128,128]{1,0:T(8,128)S(1)}, f32[128,128]{1,0:T(8,128)S(1)}, u32[]{:S(2)}, u32[]{:S(2)}) collective-permute-start(f32[128,128]{1,0:T(8,128)S(1)} %zsum.1.mine), channel_id=1, source_target_pairs={{0,4},{4,0},{1,5},{5,1},{2,6},{6,2},{3,7},{7,3},{8,12},{12,8},{9,1... | collective-permute-start | bytes 196616 | tf_op jit(solution)/shard_map/ppermute | solution.py:280
  81.3 0.9 collective-permute-done.3.other
  82.2 1.3 %gram.1 = (f32[64,256]{1,0:T(8,128)}, f32[128,256]{1,0:T(8,128)S(1)}) custom-call(s32[2]{0:T(128)S(1)} %pad_add_fusion.ids.refs_0_, f32[128,128]{1,0:T(8,128)S(1)} %zsum.1.mine, f32[128,128]{1,0:T(8,128)S(1)} %collective-permute-done.3.other), custom_call_target="tpu_custom_call" | custom-call | tf_op jit(solution)/shard_map/gram/pallas_call | solution.py:281
  83.5 10.5 %all_to_all.27.refs_0_ = f32[16,8,256]{2,1,0:T(8,128)S(1)} all-to-all(f32[16,8,256]{2,1,0:T(8,128)S(1)} %bitcast.18), channel_id=1, replica_groups=mesh['x'=4,'zh'=4,'z0'=2,'core'=2,'y'=4] {'x','y'}, dimensions={0} | all-to-all | bytes 262144 | tf_op jit(solution)/shard_map/all_to_all | solution.py:301
  94.1 9.7 %all_to_all.28.refs_0_ = f32[8,8,256]{2,1,0:T(8,128)S(1)} all-to-all(f32[8,8,256]{2,1,0:T(8,128)S(1)} %sum_xy.1), channel_id=1, replica_groups=mesh['x'=4,'zh'=4,'z0'=2,'core'=2,'y'=4] {'zh','z0'}, dimensions={0} | all-to-all | bytes 131072 | tf_op jit(solution)/shard_map/all_to_all | solution.py:303
  103.8 15.2 %all_to_all.29 = f32[32,8,256]{2,1,0:T(8,128)S(1)} all-to-all(f32[32,8,256]{2,1,0:T(8,128)S(1)} %sum_z.1), channel_id=1, replica_groups=mesh['x'=4,'zh'=4,'z0'=2,'core'=2,'y'=4] {'core','x','y'}, dimensions={0} | all-to-all | bytes 524288 | tf_op jit(solution)/shard_map/all_to_all | solution.py:305
  119.0 8.5 %factor.1 = f32[256,256]{1,0:T(8,128)} custom-call(f32[256,256]{1,0:T(8,128)S(1)} %bitcast.17), custom_call_target="tpu_custom_call" | custom-call | tf_op jit(solution)/shard_map/factor/pallas_call | solution.py:306
  (2 shorter events, 0.0 us)
Async XLA Ops:
  0.6 14.6 %copy-start.2 = (s32[64]{0:T(128)S(1)}, s32[64]{0:T(128)}, u32[]{:S(2)}) copy-start(s32[64]{0:T(128)} %param.5) | copy-start | bytes 772
  0.6 11.6 %collective-permute-start = (s32[64]{0:T(128)}, s32[64]{0:T(128)S(1)}, u32[]{:S(2)}, u32[]{:S(2)}) collective-permute-start(s32[64]{0:T(128)} %param.5), channel_id=1, source_target_pairs={{0,16},{16,0},{32,48},{48,32},{1,17},{17,1},{33,49},{49,33},{2,18}... | collective-permute-start | bytes 776 | tf_op jit(solution)/shard_map/ppermute | solution.py:237
  4.5 7.7 %collective-permute-start.2 = (s32[64]{0:T(128)}, s32[64]{0:T(128)S(1)}, u32[]{:S(2)}, u32[]{:S(2)}) collective-permute-start(s32[64]{0:T(128)} %param.5), channel_id=1, source_target_pairs={{0,48},{16,32},{32,16},{48,0},{1,49},{17,33},{33,17},{49,1},{2,50}... | collective-permute-start | bytes 776 | tf_op jit(solution)/shard_map/ppermute | solution.py:237
  8.7 6.4 %collective-permute-start.1 = (s32[64]{0:T(128)}, s32[64]{0:T(128)S(1)}, u32[]{:S(2)}, u32[]{:S(2)}) collective-permute-start(s32[64]{0:T(128)} %param.5), channel_id=1, source_target_pairs={{0,32},{16,48},{32,0},{48,16},{1,33},{17,49},{33,1},{49,17},{2,34}... | collective-permute-start | bytes 776 | tf_op jit(solution)/shard_map/ppermute | solution.py:237
  9.7 1.2 copy-start
  11.0 0.7 copy-start.1
  78.0 4.2 %collective-permute-start.3 = (f32[128,128]{1,0:T(8,128)S(1)}, f32[128,128]{1,0:T(8,128)S(1)}, u32[]{:S(2)}, u32[]{:S(2)}) collective-permute-start(f32[128,128]{1,0:T(8,128)S(1)} %zsum.1.mine), channel_id=1, source_target_pairs={{0,4},{4,0},{1,5},{5,1},{2,6},{6,2},{3,7},{7,3},{8,12},{12,8},{9,1... | collective-permute-start | bytes 196616 | tf_op jit(solution)/shard_map/ppermute | solution.py:280

commit v4 on v3

--- a/solution.py
+++ b/solution.py
@@ -20,6 +20,7 @@
 CHUNK = OUTER * 8 + 2
 CHIPS = NZH * NZ0 * NX * NY
 LANES = 128
+LINE = (0, 2, 1, 3)
 F32 = jnp.float32
 HIGHEST = lax.Precision.HIGHEST
 VMEM = pl.BlockSpec(memory_space=pltpu.VMEM)
@@ -81,15 +82,15 @@
             out[spot : spot + 8, :] = jnp.where(sub < 4, low, pltpu.roll(high, 4, 0))
             spot += CHUNK
             out[spot : spot + 8, :] = jnp.where(sub < 4, pltpu.roll(low, 4, 0), high)
-    zh = ids[0]
+    zh, c = ids[0], ids[1]
     row = lax.broadcasted_iota(jnp.int32, (2, LANES), 0)
     lane = lax.broadcasted_iota(jnp.int32, (2, LANES), 1)
     tile = jnp.zeros((2, LANES), F32)
-    for d, ref in enumerate((p0, p1, p2, p3)):
+    for d, ref in zip(LINE, (p0, p1, p2, p3)):
         place = zh ^ d
         value = (ref[...] & (ROWS - 1)).astype(F32)
         value = jnp.broadcast_to(jnp.concatenate([value, value], axis=1), (2, LANES))
-        here = (row == (place >> 1)) & ((lane >> 6) == (place & 1))
+        here = (row == (place >> 1)) & ((lane >> 6) == ((place & 1) ^ c))
         tile = jnp.where(here, value, tile)
     for k in range(GROUP):
         out[k * CHUNK + OUTER * 8 : (k + 1) * CHUNK, :] = tile
@@ -129,16 +130,17 @@
                     same = ((index & LANES) != 0) == upper
                     picked.append(jnp.where(same, level[0], pltpu.roll(level[0], 4, 0)))
                 rows.append(jnp.where(upper, picked[1], picked[0]))
-            turned = [pltpu.roll(row, SAMP, 1) for row in rows]
-            out[z0, 2 * zp, spot : spot + 8, :] = jnp.where(first, rows[0], turned[1])
-            out[z0, 2 * zp + 1, spot : spot + 8, :] = jnp.where(first, turned[0], rows[1])
+            out[z0, 2 * zp, spot : spot + 8, :] = jnp.where(first, rows[0], rows[1])
+            out[z0, 2 * zp + 1, spot : spot + 8, :] = jnp.where(first, rows[1], rows[0])
 
 
 def zsum_kernel(scale, ids, blocks, out):
     zh = ids[0]
     for z0 in range(NZ0):
         parts = [blocks[z0, d] * (parity_sign(zh & d) * scale) for d in range(NZH)]
-        out[z0 * NQ * COLS : (z0 + 1) * NQ * COLS, :] = total(parts)
+        value = total(parts)
+        value = jnp.where((zh & 1) == 1, pltpu.roll(value, SAMP, 1), value)
+        out[z0 * NQ * COLS : (z0 + 1) * NQ * COLS, :] = value
 
 
 def gram_kernel(ids, mine, other, sketch, gram, both, turned):
@@ -203,19 +205,15 @@
         first = top // block * block
         last = first + block
         if top + 8 < last:
-            solved = [None] * 8
-            for k in reversed(range(8)):
-                solved[k] = {}
-                for t in spans:
-                    value = rows[k][t]
-                    for i in range(7, k, -1):
-                        value = value - head[k][i] * solved[i][t]
-                    solved[k][t] = value * inverse[k]
             for g in range(top + 8, last, 8):
                 left = work[g : g + 8, spans[tile]]
                 sides = [jnp.broadcast_to(left[:, at + j : at + j + 1], (8, LANES)) for j in range(8)]
+                for k in range(8):
+                    sides[k] = sides[k] * inverse[k]
+                    for j in range(k + 1, 8):
+                        sides[j] = sides[j] - sides[k] * head[k][j]
                 for t, span in spans.items():
-                    work[g : g + 8, span] = work[g : g + 8, span] - total([sides[j] * solved[j][t] for j in range(8)])
+                    work[g : g + 8, span] = work[g : g + 8, span] - total([sides[k] * rows[k][t] for k in range(8)])
         elif last < W:
             start = last // LANES * LANES
             done = factor[first:last, start:]
@@ -252,7 +250,7 @@
         out_specs=VMEM,
         compiler_params=params(16),
         name="pack",
-    )(ids, table, *line)
+    )(ids, table, *[line[d] for d in LINE])
     packed = packed.reshape(GROUP, CHUNK // 2, 2, LANES)
     packed = lax.all_to_all(packed, ("z0", "core", "x", "y"), 0, 0, tiled=True).reshape(GROUP * CHUNK, LANES)
 

time: 128 us -> 125 us (0.977)
  Pallas kernels: 15.8 us -> 13.5 us
  waiting for transfers between devices: 3.83 us -> 1.75 us
  blocking collectives: 92.8 us -> 94.8 us
    all_to_all x1, blocking collectives: 16.8 us -> 19.2 us  [on_device(): lax.all_to_all(sampled.reshape(CHIPS, COLS, LANES), ('z0', 'zh', 'x', 'y'...]
    ppermute x3, waiting for transfers between devices: 2.92 us -> 0.85 us  [on_device(): lax.ppermute(picks, 'zh', [(i, i ^ d) for i in range(NZH)])]
    pallas_call x1, Pallas kernels: 4.14 us -> 2.38 us  [on_device(): pl.pallas_call(gather_kernel, out_shape=shape(NZ0, NZH, NQ * COLS, LANES)...]
where the time goes in v4:
time: 125 us
  blocking collectives  94.8 us (76%)
  Pallas kernels  13.5 us (11%)
  starting transfers between devices  12.4 us (10%)
  local copies, waits for them, and re-layouts  1.92 us (2%)
  waiting for transfers between devices  1.75 us (1%)
    all_to_all x1, blocking collectives, on_device(): lax.all_to_all(packed, ('z0', 'core', 'x', 'y'), 0, 0, tiled=True)  40.2 us
    all_to_all x1, blocking collectives, on_device(): lax.all_to_all(sampled.reshape(CHIPS, COLS, LANES), ('z0', 'zh', 'x', 'y'...  19.2 us
    all_to_all x1, blocking collectives, on_device(): lax.all_to_all(rows, ('core', 'x', 'y'), 0, 0, tiled=True).reshape(W, W)  15.2 us
    all_to_all x1, blocking collectives, on_device(): gram = lax.all_to_all(gram.reshape(NQ, 8, W), ('x', 'y'), 0, 0, tiled=True)  10.5 us
    all_to_all x1, blocking collectives, on_device(): rows = lax.all_to_all(rows, ('zh', 'z0'), 0, 0, tiled=True)  9.71 us
    ppermute x3, starting transfers between devices, on_device(): lax.ppermute(picks, 'zh', [(i, i ^ d) for i in range(NZH)])  9.02 us
    pallas_call x1, Pallas kernels, on_device(): pl.pallas_call(factor_kernel, out_shape=shape(W, W), in_specs=[VMEM], out...  7.84 us
    ppermute x1, starting transfers between devices, on_device(): other = lax.ppermute(mine, 'core', [(0, 1), (1, 0)])  3.35 us
  transfers between devices with their start and end apart: 4, of which 2 were waited for; matrix products, arithmetic and copies ran while one was open for 0% of the time, Pallas kernels for 0%

profile of v4, /device:TPU:1, one launch (start us, length us, event | category | flops | bytes accessed | tf_op | source)
XLA Modules:
  0.0 125.1 jit_solution(7371372658784114821)
XLA Ops:
  0.6 0.0 copy-start.2
  0.6 7.8 %collective-permute-start = (s32[64]{0:T(128)}, s32[64]{0:T(128)S(1)}, u32[]{:S(2)}, u32[]{:S(2)}) collective-permute-start(s32[64]{0:T(128)} %param.5), channel_id=1, source_target_pairs={{0,32},{16,48},{32,0},{48,16},{1,33},{17,49},{33,1},{49,17},{2,34}... | collective-permute-start | bytes 776 | tf_op jit(solution)/shard_map/ppermute | solution.py:235
  8.5 0.0 collective-permute-start.2
  8.5 1.2 collective-permute-start.1
  9.7 0.1 pad_add_fusion.ids.refs_0_
  9.7 0.0 copy-start
  9.7 1.2 copy-done
  11.0 0.0 copy-start.1
  11.0 0.7 copy-done.1
  11.7 0.6 local.1.table
  12.2 0.0 collective-permute-done
  12.3 0.8 collective-permute-done.2
  13.1 0.0 collective-permute-done.1
  13.1 0.0 copy-done.2
  13.1 0.7 pack.1
  13.8 40.2 %all_to_all.25 = f32[64,33,2,128]{3,2,1,0:T(2,128)S(1)} all-to-all(f32[64,33,2,128]{3,2,1,0:T(2,128)S(1)} %bitcast.13), channel_id=1, replica_groups=mesh['x'=4,'zh'=4,'z0'=2,'core'=2,'y'=4] {'z0','core','x','y'}, dimensions={0} | all-to-all | bytes 4325376 | tf_op jit(solution)/shard_map/all_to_all | solution.py:255
  54.1 2.4 %gather.1 = f32[2,4,64,128]{3,2,1,0:T(8,128)S(1)} custom-call(f32[4224,128]{1,0:T(8,128)S(1)} %bitcast.14), custom_call_target="tpu_custom_call" | custom-call | tf_op jit(solution)/shard_map/gather/pallas_call | solution.py:257
  56.5 19.2 %all_to_all.26 = f32[128,4,128]{2,1,0:T(4,128)S(1)} all-to-all(f32[128,4,128]{2,1,0:T(4,128)S(1)} %bitcast.15), channel_id=1, replica_groups=mesh['x'=4,'zh'=4,'z0'=2,'core'=2,'y'=4] {'z0','zh','x','y'}, dimensions={0} | all-to-all | bytes 524288 | tf_op jit(solution)/shard_map/all_to_all | solution.py:266
  75.6 0.6 zsum.1.mine
  76.3 3.3 %collective-permute-start.3 = (f32[128,128]{1,0:T(8,128)S(1)}, f32[128,128]{1,0:T(8,128)S(1)}, u32[]{:S(2)}, u32[]{:S(2)}) collective-permute-start(f32[128,128]{1,0:T(8,128)S(1)} %zsum.1.mine), channel_id=1, source_target_pairs={{0,4},{4,0},{1,5},{5,1},{2,6},{6,2},{3,7},{7,3},{8,12},{12,8},{9,1... | collective-permute-start | bytes 196616 | tf_op jit(solution)/shard_map/ppermute | solution.py:278
  79.6 0.9 collective-permute-done.3.other
  80.5 1.3 %gram.1 = (f32[64,256]{1,0:T(8,128)}, f32[128,256]{1,0:T(8,128)S(1)}) custom-call(s32[2]{0:T(128)S(1)} %pad_add_fusion.ids.refs_0_, f32[128,128]{1,0:T(8,128)S(1)} %zsum.1.mine, f32[128,128]{1,0:T(8,128)S(1)} %collective-permute-done.3.other), custom_call_target="tpu_custom_call" | custom-call | tf_op jit(solution)/shard_map/gram/pallas_call | solution.py:279
  81.8 10.5 %all_to_all.27.refs_0_ = f32[16,8,256]{2,1,0:T(8,128)S(1)} all-to-all(f32[16,8,256]{2,1,0:T(8,128)S(1)} %bitcast.18), channel_id=1, replica_groups=mesh['x'=4,'zh'=4,'z0'=2,'core'=2,'y'=4] {'x','y'}, dimensions={0} | all-to-all | bytes 262144 | tf_op jit(solution)/shard_map/all_to_all | solution.py:299
  92.4 9.7 %all_to_all.28.refs_0_ = f32[8,8,256]{2,1,0:T(8,128)S(1)} all-to-all(f32[8,8,256]{2,1,0:T(8,128)S(1)} %sum_xy.1), channel_id=1, replica_groups=mesh['x'=4,'zh'=4,'z0'=2,'core'=2,'y'=4] {'zh','z0'}, dimensions={0} | all-to-all | bytes 131072 | tf_op jit(solution)/shard_map/all_to_all | solution.py:301
  102.1 15.2 %all_to_all.29 = f32[32,8,256]{2,1,0:T(8,128)S(1)} all-to-all(f32[32,8,256]{2,1,0:T(8,128)S(1)} %sum_z.1), channel_id=1, replica_groups=mesh['x'=4,'zh'=4,'z0'=2,'core'=2,'y'=4] {'core','x','y'}, dimensions={0} | all-to-all | bytes 524288 | tf_op jit(solution)/shard_map/all_to_all | solution.py:303
  117.3 7.8 %factor.1 = f32[256,256]{1,0:T(8,128)} custom-call(f32[256,256]{1,0:T(8,128)S(1)} %bitcast.17), custom_call_target="tpu_custom_call" | custom-call | tf_op jit(solution)/shard_map/factor/pallas_call | solution.py:304
  (2 shorter events, 0.0 us)
Async XLA Ops:
  0.6 12.5 %copy-start.2 = (s32[64]{0:T(128)S(1)}, s32[64]{0:T(128)}, u32[]{:S(2)}) copy-start(s32[64]{0:T(128)} %param.5) | copy-start | bytes 772
  0.6 11.6 %collective-permute-start = (s32[64]{0:T(128)}, s32[64]{0:T(128)S(1)}, u32[]{:S(2)}, u32[]{:S(2)}) collective-permute-start(s32[64]{0:T(128)} %param.5), channel_id=1, source_target_pairs={{0,32},{16,48},{32,0},{48,16},{1,33},{17,49},{33,1},{49,17},{2,34}... | collective-permute-start | bytes 776 | tf_op jit(solution)/shard_map/ppermute | solution.py:235
  8.5 4.6 %collective-permute-start.2 = (s32[64]{0:T(128)}, s32[64]{0:T(128)S(1)}, u32[]{:S(2)}, u32[]{:S(2)}) collective-permute-start(s32[64]{0:T(128)} %param.5), channel_id=1, source_target_pairs={{0,48},{16,32},{32,16},{48,0},{1,49},{17,33},{33,17},{49,1},{2,50}... | collective-permute-start | bytes 776 | tf_op jit(solution)/shard_map/ppermute | solution.py:235
  8.5 4.6 %collective-permute-start.1 = (s32[64]{0:T(128)}, s32[64]{0:T(128)S(1)}, u32[]{:S(2)}, u32[]{:S(2)}) collective-permute-start(s32[64]{0:T(128)} %param.5), channel_id=1, source_target_pairs={{0,16},{16,0},{32,48},{48,32},{1,17},{17,1},{33,49},{49,33},{2,18}... | collective-permute-start | bytes 776 | tf_op jit(solution)/shard_map/ppermute | solution.py:235
  9.7 1.2 copy-start
  11.0 0.7 copy-start.1
  76.3 4.2 %collective-permute-start.3 = (f32[128,128]{1,0:T(8,128)S(1)}, f32[128,128]{1,0:T(8,128)S(1)}, u32[]{:S(2)}, u32[]{:S(2)}) collective-permute-start(f32[128,128]{1,0:T(8,128)S(1)} %zsum.1.mine), channel_id=1, source_target_pairs={{0,4},{4,0},{1,5},{5,1},{2,6},{6,2},{3,7},{7,3},{8,12},{12,8},{9,1... | collective-permute-start | bytes 196616 | tf_op jit(solution)/shard_map/ppermute | solution.py:278

commit v5 on v4

--- a/solution.py
+++ b/solution.py
@@ -24,7 +24,6 @@
 F32 = jnp.float32
 HIGHEST = lax.Precision.HIGHEST
 VMEM = pl.BlockSpec(memory_space=pltpu.VMEM)
-SMEM = pl.BlockSpec(memory_space=pltpu.SMEM)
 
 
 def params(mib):
@@ -82,7 +81,7 @@
             out[spot : spot + 8, :] = jnp.where(sub < 4, low, pltpu.roll(high, 4, 0))
             spot += CHUNK
             out[spot : spot + 8, :] = jnp.where(sub < 4, pltpu.roll(low, 4, 0), high)
-    zh, c = ids[0], ids[1]
+    zh, c = ids[0:1, :], ids[1:2, :]
     row = lax.broadcasted_iota(jnp.int32, (2, LANES), 0)
     lane = lax.broadcasted_iota(jnp.int32, (2, LANES), 1)
     tile = jnp.zeros((2, LANES), F32)
@@ -135,28 +134,32 @@
 
 
 def zsum_kernel(scale, ids, blocks, out):
-    zh = ids[0]
+    zh = ids[0:1, :]
+    odd = jnp.broadcast_to(zh, (8, LANES)) & 1 == 1
+    signs = [jnp.broadcast_to(parity_sign(zh & d) * scale, (8, LANES)) for d in range(NZH)]
     for z0 in range(NZ0):
-        parts = [blocks[z0, d] * (parity_sign(zh & d) * scale) for d in range(NZH)]
-        value = total(parts)
-        value = jnp.where((zh & 1) == 1, pltpu.roll(value, SAMP, 1), value)
-        out[z0 * NQ * COLS : (z0 + 1) * NQ * COLS, :] = value
-
-
-def gram_kernel(ids, mine, other, sketch, gram, both, turned):
-    c = ids[1]
+        for spot in range(0, NQ * COLS, 8):
+            value = total([blocks[z0, d, spot : spot + 8, :] * signs[d] for d in range(NZH)])
+            value = jnp.where(odd, pltpu.roll(value, SAMP, 1), value)
+            out[z0 * NQ * COLS + spot : z0 * NQ * COLS + spot + 8, :] = value
+
+
+def gram_kernel(ids, mine, other, sketch, gram):
     part = NQ * COLS
+    zero = jnp.broadcast_to(ids[1:2, :], (part, LANES)) == 0
+    pieces = []
     for z0 in range(NZ0):
-        rows = slice(z0 * part, (z0 + 1) * part)
-        both[pl.ds(pl.multiple_of((z0 * NC + c) * part, part), part), :] = mine[rows, :]
-        both[pl.ds(pl.multiple_of((z0 * NC + 1 - c) * part, part), part), :] = other[rows, :]
-    value = both[...]
-    turned[...] = value.T
-    sketch[...] = turned[pl.ds(pl.multiple_of(c * SAMP, SAMP), SAMP), :]
-    half = both[pl.ds(pl.multiple_of(c * 128, 128), 128), :]
+        a, b = mine[z0 * part : (z0 + 1) * part, :], other[z0 * part : (z0 + 1) * part, :]
+        pieces += [jnp.where(zero, a, b), jnp.where(zero, b, a)]
+    low, high = jnp.concatenate(pieces[:2], axis=0), jnp.concatenate(pieces[2:], axis=0)
+    value = jnp.concatenate([low, high], axis=0)
+    zero = jnp.broadcast_to(ids[1:2, :], (W // NC, LANES)) == 0
     gram[...] = lax.dot_general(
-        half, value, (((1,), (1,)), ((), ())), precision=HIGHEST, preferred_element_type=F32
+        jnp.where(zero, low, high), value, (((1,), (1,)), ((), ())), precision=HIGHEST, preferred_element_type=F32
     )
+    for tile, block in enumerate((low, high)):
+        turned = block.T
+        sketch[:, tile * LANES : (tile + 1) * LANES] = jnp.where(zero[:SAMP], turned[:SAMP], turned[SAMP:])
 
 
 def spread_kernel(scale, blocks, out):
@@ -165,11 +168,12 @@
         out[k] = value
 
 
-def factor_kernel(gram, factor, work):
+def factor_kernel(gram, rows_in, factor, rows_out, work):
+    rows_out[...] = rows_in[...]
     work[...] = gram[...]
     sub = lax.broadcasted_iota(jnp.int32, (8, LANES), 0)
     lane = lax.broadcasted_iota(jnp.int32, (8, LANES), 1)
-    block = 32
+    block = 64
     for top in range(0, W, 8):
         at, tile = top % LANES, top // LANES
         spans = {t: slice(t * LANES, (t + 1) * LANES) for t in range(tile, W // LANES)}
@@ -230,7 +234,7 @@
 
 def on_device(matrix, signs, picks):
     zh, c = lax.axis_index("zh"), lax.axis_index("core")
-    ids = jnp.stack([zh, c]).astype(jnp.int32)
+    ids = jnp.broadcast_to(jnp.stack([zh, c]).astype(jnp.int32)[:, None], (2, LANES))
     matrix, ids = lax.optimization_barrier((matrix, ids))
     line = [picks] + [lax.ppermute(picks, "zh", [(i, i ^ d) for i in range(NZH)]) for d in range(1, NZH)]
     line = [value.reshape(1, SAMP) for value in line]
@@ -246,7 +250,7 @@
     packed = pl.pallas_call(
         pack_kernel,
         out_shape=shape(GROUP * CHUNK, LANES),
-        in_specs=[SMEM] + [VMEM] * 5,
+        in_specs=[VMEM] * 6,
         out_specs=VMEM,
         compiler_params=params(16),
         name="pack",
@@ -270,7 +274,7 @@
     mine = pl.pallas_call(
         lambda *refs: zsum_kernel(1.0 / math.sqrt(ROWS * 256), *refs),
         out_shape=shape(128, LANES),
-        in_specs=[SMEM, VMEM],
+        in_specs=[VMEM, VMEM],
         out_specs=VMEM,
         compiler_params=params(4),
         name="zsum",
@@ -279,9 +283,8 @@
     sketch, gram = pl.pallas_call(
         gram_kernel,
         out_shape=[shape(SAMP, W), shape(W // NC, W)],
-        in_specs=[SMEM, VMEM, VMEM],
+        in_specs=[VMEM, VMEM, VMEM],
         out_specs=[VMEM, VMEM],
-        scratch_shapes=[pltpu.VMEM((W, 128), F32), pltpu.VMEM((128, W), F32)],
         compiler_params=params(4),
         name="gram",
     )(ids, mine, other)
@@ -301,15 +304,15 @@
     rows = lax.all_to_all(rows, ("zh", "z0"), 0, 0, tiled=True)
     rows = spread(rows, NC * NQ, 1.0 / (SAMP * 256), "sum_z")
     gram = lax.all_to_all(rows, ("core", "x", "y"), 0, 0, tiled=True).reshape(W, W)
-    factor = pl.pallas_call(
+    factor, sketch = pl.pallas_call(
         factor_kernel,
-        out_shape=shape(W, W),
-        in_specs=[VMEM],
-        out_specs=VMEM,
+        out_shape=[shape(W, W), shape(SAMP, W)],
+        in_specs=[VMEM, VMEM],
+        out_specs=[VMEM, VMEM],
         scratch_shapes=[pltpu.VMEM((W, W), F32)],
         compiler_params=params(4),
         name="factor",
-    )(gram)
+    )(gram, sketch)
     return (sketch, factor)
 
 

time: 125 us -> 122 us (0.976)
  Pallas kernels: 13.5 us -> 10.2 us
where the time goes in v5:
time: 122 us
  blocking collectives  94.8 us (78%)
  starting transfers between devices  12.4 us (10%)
  Pallas kernels  10.2 us (8%)
  local copies, waits for them, and re-layouts  2 us (2%)
  waiting for transfers between devices  1.68 us (1%)
    all_to_all x1, blocking collectives, on_device(): lax.all_to_all(packed, ('z0', 'core', 'x', 'y'), 0, 0, tiled=True)  40.2 us
    all_to_all x1, blocking collectives, on_device(): lax.all_to_all(sampled.reshape(CHIPS, COLS, LANES), ('z0', 'zh', 'x', 'y'...  19.2 us
    all_to_all x1, blocking collectives, on_device(): lax.all_to_all(rows, ('core', 'x', 'y'), 0, 0, tiled=True).reshape(W, W)  15.2 us
    all_to_all x1, blocking collectives, on_device(): gram = lax.all_to_all(gram.reshape(NQ, 8, W), ('x', 'y'), 0, 0, tiled=True)  10.5 us
    all_to_all x1, blocking collectives, on_device(): rows = lax.all_to_all(rows, ('zh', 'z0'), 0, 0, tiled=True)  9.71 us
    ppermute x3, starting transfers between devices, on_device(): lax.ppermute(picks, 'zh', [(i, i ^ d) for i in range(NZH)])  9.02 us
    pallas_call x1, Pallas kernels, on_device(): pl.pallas_call(factor_kernel, out_shape=[shape(W, W), shape(SAMP, W)], in...  6.71 us
    ppermute x1, starting transfers between devices, on_device(): other = lax.ppermute(mine, 'core', [(0, 1), (1, 0)])  3.35 us
  transfers between devices with their start and end apart: 4, of which 2 were waited for; matrix products, arithmetic and copies ran while one was open for 0% of the time, Pallas kernels for 0%

profile of v5, /device:TPU:1, one launch (start us, length us, event | category | flops | bytes accessed | tf_op | source)
XLA Modules:
  0.0 121.9 jit_solution(2175615893389964426)
XLA Ops:
  0.6 0.0 copy-start.2
  0.6 7.8 %collective-permute-start = (s32[64]{0:T(128)}, s32[64]{0:T(128)S(1)}, u32[]{:S(2)}, u32[]{:S(2)}) collective-permute-start(s32[64]{0:T(128)} %param.5), channel_id=1, source_target_pairs={{0,32},{16,48},{32,0},{48,16},{1,33},{17,49},{33,1},{49,17},{2,34}... | collective-permute-start | bytes 776 | tf_op jit(solution)/shard_map/ppermute | solution.py:239
  8.5 0.0 collective-permute-start.2
  8.5 1.2 collective-permute-start.1
  9.7 0.1 pad_add_fusion
  9.7 0.1 broadcast_in_dim.2.ids.refs_0_
  9.8 0.0 copy-start
  9.8 1.2 %copy-done = bf16[2048,256]{1,0:T(8,128)(2,1)S(1)} copy-done((bf16[2048,256]{1,0:T(8,128)(2,1)S(1)}, bf16[2048,256]{1,0:T(8,128)(2,1)}, u32[]{:S(2)}) %copy-start) | copy-done | bytes 1048600
  11.0 0.0 copy-start.1
  11.0 0.7 copy-done.1
  11.7 0.6 local.1.table
  12.3 0.0 collective-permute-done
  12.3 0.8 collective-permute-done.2
  13.1 0.0 collective-permute-done.1
  13.1 0.0 copy-done.2
  13.1 0.2 pack.1
  13.3 40.2 %all_to_all.25 = f32[64,33,2,128]{3,2,1,0:T(2,128)S(1)} all-to-all(f32[64,33,2,128]{3,2,1,0:T(2,128)S(1)} %bitcast.13), channel_id=1, replica_groups=mesh['x'=4,'zh'=4,'z0'=2,'core'=2,'y'=4] {'z0','core','x','y'}, dimensions={0} | all-to-all | bytes 4325376 | tf_op jit(solution)/shard_map/all_to_all | solution.py:259
  53.5 2.4 %gather.1 = f32[2,4,64,128]{3,2,1,0:T(8,128)S(1)} custom-call(f32[4224,128]{1,0:T(8,128)S(1)} %bitcast.14), custom_call_target="tpu_custom_call" | custom-call | tf_op jit(solution)/shard_map/gather/pallas_call | solution.py:261
  55.9 19.2 %all_to_all.26 = f32[128,4,128]{2,1,0:T(4,128)S(1)} all-to-all(f32[128,4,128]{2,1,0:T(4,128)S(1)} %bitcast.15), channel_id=1, replica_groups=mesh['x'=4,'zh'=4,'z0'=2,'core'=2,'y'=4] {'z0','zh','x','y'}, dimensions={0} | all-to-all | bytes 524288 | tf_op jit(solution)/shard_map/all_to_all | solution.py:270
  75.1 0.1 zsum.1.mine
  75.2 3.3 %collective-permute-start.3 = (f32[128,128]{1,0:T(8,128)S(1)}, f32[128,128]{1,0:T(8,128)S(1)}, u32[]{:S(2)}, u32[]{:S(2)}) collective-permute-start(f32[128,128]{1,0:T(8,128)S(1)} %zsum.1.mine), channel_id=1, source_target_pairs={{0,4},{4,0},{1,5},{5,1},{2,6},{6,2},{3,7},{7,3},{8,12},{12,8},{9,1... | collective-permute-start | bytes 196616 | tf_op jit(solution)/shard_map/ppermute | solution.py:282
  78.5 0.9 collective-permute-done.3.other
  79.4 0.3 gram.1
  79.7 10.5 %all_to_all.27.refs_0_ = f32[16,8,256]{2,1,0:T(8,128)S(1)} all-to-all(f32[16,8,256]{2,1,0:T(8,128)S(1)} %bitcast.18), channel_id=1, replica_groups=mesh['x'=4,'zh'=4,'z0'=2,'core'=2,'y'=4] {'x','y'}, dimensions={0} | all-to-all | bytes 262144 | tf_op jit(solution)/shard_map/all_to_all | solution.py:302
  90.3 9.7 %all_to_all.28.refs_0_ = f32[8,8,256]{2,1,0:T(8,128)S(1)} all-to-all(f32[8,8,256]{2,1,0:T(8,128)S(1)} %sum_xy.1), channel_id=1, replica_groups=mesh['x'=4,'zh'=4,'z0'=2,'core'=2,'y'=4] {'zh','z0'}, dimensions={0} | all-to-all | bytes 131072 | tf_op jit(solution)/shard_map/all_to_all | solution.py:304
  100.0 15.2 %all_to_all.29 = f32[32,8,256]{2,1,0:T(8,128)S(1)} all-to-all(f32[32,8,256]{2,1,0:T(8,128)S(1)} %sum_z.1), channel_id=1, replica_groups=mesh['x'=4,'zh'=4,'z0'=2,'core'=2,'y'=4] {'core','x','y'}, dimensions={0} | all-to-all | bytes 524288 | tf_op jit(solution)/shard_map/all_to_all | solution.py:306
  115.2 6.7 %factor.1 = (f32[256,256]{1,0:T(8,128)}, f32[64,256]{1,0:T(8,128)}) custom-call(f32[256,256]{1,0:T(8,128)S(1)} %bitcast.16, f32[64,256]{1,0:T(8,128)S(1)} %get-tuple-element.11.rows_in), custom_call_target="tpu_custom_call" | custom-call | tf_op jit(solution)/shard_map/factor/pallas_call | solution.py:307
  (2 shorter events, 0.0 us)
Async XLA Ops:
  0.6 12.5 %copy-start.2 = (s32[64]{0:T(128)S(1)}, s32[64]{0:T(128)}, u32[]{:S(2)}) copy-start(s32[64]{0:T(128)} %param.5) | copy-start | bytes 772
  0.6 11.7 %collective-permute-start = (s32[64]{0:T(128)}, s32[64]{0:T(128)S(1)}, u32[]{:S(2)}, u32[]{:S(2)}) collective-permute-start(s32[64]{0:T(128)} %param.5), channel_id=1, source_target_pairs={{0,32},{16,48},{32,0},{48,16},{1,33},{17,49},{33,1},{49,17},{2,34}... | collective-permute-start | bytes 776 | tf_op jit(solution)/shard_map/ppermute | solution.py:239
  8.5 4.6 %collective-permute-start.2 = (s32[64]{0:T(128)}, s32[64]{0:T(128)S(1)}, u32[]{:S(2)}, u32[]{:S(2)}) collective-permute-start(s32[64]{0:T(128)} %param.5), channel_id=1, source_target_pairs={{0,48},{16,32},{32,16},{48,0},{1,49},{17,33},{33,17},{49,1},{2,50}... | collective-permute-start | bytes 776 | tf_op jit(solution)/shard_map/ppermute | solution.py:239
  8.5 4.6 %collective-permute-start.1 = (s32[64]{0:T(128)}, s32[64]{0:T(128)S(1)}, u32[]{:S(2)}, u32[]{:S(2)}) collective-permute-start(s32[64]{0:T(128)} %param.5), channel_id=1, source_target_pairs={{0,16},{16,0},{32,48},{48,32},{1,17},{17,1},{33,49},{49,33},{2,18}... | collective-permute-start | bytes 776 | tf_op jit(solution)/shard_map/ppermute | solution.py:239
  9.8 1.2 %copy-start = (bf16[2048,256]{1,0:T(8,128)(2,1)S(1)}, bf16[2048,256]{1,0:T(8,128)(2,1)}, u32[]{:S(2)}) copy-start(bf16[2048,256]{1,0:T(8,128)(2,1)} %matrix) | copy-start | bytes 3145732
  11.0 0.7 copy-start.1
  75.2 4.2 %collective-permute-start.3 = (f32[128,128]{1,0:T(8,128)S(1)}, f32[128,128]{1,0:T(8,128)S(1)}, u32[]{:S(2)}, u32[]{:S(2)}) collective-permute-start(f32[128,128]{1,0:T(8,128)S(1)} %zsum.1.mine), channel_id=1, source_target_pairs={{0,4},{4,0},{1,5},{5,1},{2,6},{6,2},{3,7},{7,3},{8,12},{12,8},{9,1... | collective-permute-start | bytes 196616 | tf_op jit(solution)/shard_map/ppermute | solution.py:282

commit v6 on v5

--- a/solution.py
+++ b/solution.py
@@ -95,7 +95,7 @@
         out[k * CHUNK + OUTER * 8 : (k + 1) * CHUNK, :] = tile
 
 
-def gather_kernel(blocks, out, table):
+def gather_kernel(ids, blocks, out, table):
     for high in range(32):
         values = [blocks[(high * 2 + low) * CHUNK + o * 8 : (high * 2 + low) * CHUNK + o * 8 + 8, :] for low in range(2) for o in range(OUTER)]
         for k, value in enumerate(butterfly(values)):
@@ -107,6 +107,8 @@
     sub = lax.broadcasted_iota(jnp.int32, (8, LANES), 0)
     lane = lax.broadcasted_iota(jnp.int32, (8, LANES), 1)
     upper, first = sub >= 4, lane < SAMP
+    zh, half_lane = ids[0:1, :], lane[0:1, :] >> 6
+    far = [[((zh >> 1) != zp) & (half_lane == ((zh & 1) ^ c)) for c in range(NC)] for zp in range(2)]
     for half in range(GROUP // 4):
         z0, spot = half // (NQ // 2), half % (NQ // 2) * 8
         for zp in range(2):
@@ -116,7 +118,9 @@
                 for ylo in range(2):
                     device = (z0 * NC + c) * NQ + spot // 4 + ylo
                     row = device * CHUNK + OUTER * 8 + zp
-                    index = blocks[row : row + 1, :].astype(jnp.int32)
+                    cross = row + (1 - 2 * z0) * NC * NQ * CHUNK
+                    index = jnp.where(far[zp][c], blocks[cross : cross + 1, :], blocks[row : row + 1, :])
+                    index = index.astype(jnp.int32)
                     index = jnp.broadcast_to(index, (8, LANES))
                     low = index & (LANES - 1)
                     level = [
@@ -236,8 +240,9 @@
     zh, c = lax.axis_index("zh"), lax.axis_index("core")
     ids = jnp.broadcast_to(jnp.stack([zh, c]).astype(jnp.int32)[:, None], (2, LANES))
     matrix, ids = lax.optimization_barrier((matrix, ids))
-    line = [picks] + [lax.ppermute(picks, "zh", [(i, i ^ d) for i in range(NZH)]) for d in range(1, NZH)]
-    line = [value.reshape(1, SAMP) for value in line]
+    near = [lax.ppermute(picks, "zh", [(i, i ^ d) for i in range(NZH)]) for d in (1, 3)]
+    far = lax.ppermute(picks, ("zh", "z0"), [(i, (i + 3 if i & 1 else i - 3) % NZ) for i in range(NZ)])
+    line = [value.reshape(1, SAMP) for value in (picks, near[0], far, near[1])]
 
     table = pl.pallas_call(
         local_kernel,
@@ -261,12 +266,12 @@
     sampled = pl.pallas_call(
         gather_kernel,
         out_shape=shape(NZ0, NZH, NQ * COLS, LANES),
-        in_specs=[VMEM],
+        in_specs=[VMEM] * 2,
         out_specs=VMEM,
         scratch_shapes=[pltpu.VMEM((GROUP * OUTER, 8, LANES), F32)],
         compiler_params=params(16),
         name="gather",
-    )(packed)
+    )(ids, packed)
     sampled = lax.all_to_all(
         sampled.reshape(CHIPS, COLS, LANES), ("z0", "zh", "x", "y"), 0, 0, tiled=True
     ).reshape(NZ0, NZH, NQ * COLS, LANES)
@@ -301,7 +306,7 @@
 
     gram = lax.all_to_all(gram.reshape(NQ, 8, W), ("x", "y"), 0, 0, tiled=True)
     rows = spread(gram, NZ, 1.0, "sum_xy")
-    rows = lax.all_to_all(rows, ("zh", "z0"), 0, 0, tiled=True)
+    rows = lax.all_to_all(rows, ("z0", "zh"), 0, 0, tiled=True)
     rows = spread(rows, NC * NQ, 1.0 / (SAMP * 256), "sum_z")
     gram = lax.all_to_all(rows, ("core", "x", "y"), 0, 0, tiled=True).reshape(W, W)
     factor, sketch = pl.pallas_call(

time: 122 us -> 121 us (level)
    ppermute x3 -> x2, starting transfers between devices: 9.02 us -> 1.2 us  [on_device(): lax.ppermute(picks, 'zh', [(i, i ^ d) for i in range(NZH)])]
    ppermute x0 -> x1, starting transfers between devices: none -> 7.38 us  [on_device(): lax.ppermute(picks, ('zh', 'z0'), [(i, (i + 3 if i & 1 else i - 3) % NZ)...]
where the time goes in v6:
time: 121 us
  blocking collectives  94.2 us (78%)
  starting transfers between devices  11.9 us (10%)
  Pallas kernels  10.2 us (8%)
  local copies, waits for them, and re-layouts  2 us (2%)
  waiting for transfers between devices  1.68 us (1%)
    all_to_all x1, blocking collectives, on_device(): lax.all_to_all(packed, ('z0', 'core', 'x', 'y'), 0, 0, tiled=True)  40.2 us
    all_to_all x1, blocking collectives, on_device(): lax.all_to_all(sampled.reshape(CHIPS, COLS, LANES), ('z0', 'zh', 'x', 'y'...  19.2 us
    all_to_all x1, blocking collectives, on_device(): lax.all_to_all(rows, ('core', 'x', 'y'), 0, 0, tiled=True).reshape(W, W)  15.1 us
    all_to_all x1, blocking collectives, on_device(): gram = lax.all_to_all(gram.reshape(NQ, 8, W), ('x', 'y'), 0, 0, tiled=True)  10.5 us
    all_to_all x1, blocking collectives, on_device(): rows = lax.all_to_all(rows, ('z0', 'zh'), 0, 0, tiled=True)  9.14 us
    ppermute x1, starting transfers between devices, on_device(): lax.ppermute(picks, ('zh', 'z0'), [(i, (i + 3 if i & 1 else i - 3) % NZ)...  7.38 us
    pallas_call x1, Pallas kernels, on_device(): pl.pallas_call(factor_kernel, out_shape=[shape(W, W), shape(SAMP, W)], in...  6.71 us
    ppermute x1, starting transfers between devices, on_device(): other = lax.ppermute(mine, 'core', [(0, 1), (1, 0)])  3.35 us
  transfers between devices with their start and end apart: 4, of which 2 were waited for; matrix products, arithmetic and copies ran while one was open for 0% of the time, Pallas kernels for 0%

profile of v6, /device:TPU:1, one launch (start us, length us, event | category | flops | bytes accessed | tf_op | source)
XLA Modules:
  0.0 120.9 jit_solution(16330885506738378201)
XLA Ops:
  0.6 0.0 copy-start.2
  0.6 7.4 %collective-permute-start = (s32[64]{0:T(128)}, s32[64]{0:T(128)S(1)}, u32[]{:S(2)}, u32[]{:S(2)}) collective-permute-start(s32[64]{0:T(128)} %param.5), channel_id=1, source_target_pairs={{0,40},{8,32},{16,56},{24,48},{32,8},{40,0},{48,24},{56,16},{1,41}... | collective-permute-start | bytes 776 | tf_op jit(solution)/shard_map/ppermute | solution.py:244
  8.0 0.3 collective-permute-start.2
  8.3 0.9 collective-permute-start.1
  9.2 0.1 pad_add_fusion
  9.3 0.1 broadcast_in_dim.2.ids.refs_0_
  9.4 0.0 copy-start
  9.4 1.2 %copy-done = bf16[2048,256]{1,0:T(8,128)(2,1)S(1)} copy-done((bf16[2048,256]{1,0:T(8,128)(2,1)S(1)}, bf16[2048,256]{1,0:T(8,128)(2,1)}, u32[]{:S(2)}) %copy-start) | copy-done | bytes 1048600
  10.6 0.0 copy-start.1
  10.6 0.7 copy-done.1
  11.3 0.6 local.1.table
  11.9 0.0 collective-permute-done
  11.9 0.8 collective-permute-done.2
  12.7 0.0 collective-permute-done.1
  12.7 0.0 copy-done.2
  12.7 0.2 pack.1
  12.8 40.2 %all_to_all.25 = f32[64,33,2,128]{3,2,1,0:T(2,128)S(1)} all-to-all(f32[64,33,2,128]{3,2,1,0:T(2,128)S(1)} %bitcast.13), channel_id=1, replica_groups=mesh['x'=4,'zh'=4,'z0'=2,'core'=2,'y'=4] {'z0','core','x','y'}, dimensions={0} | all-to-all | bytes 4325376 | tf_op jit(solution)/shard_map/all_to_all | solution.py:264
  53.1 2.4 %gather.1 = f32[2,4,64,128]{3,2,1,0:T(8,128)S(1)} custom-call(s32[2,128]{1,0:T(2,128)S(1)} %broadcast_in_dim.2.ids.refs_0_, f32[4224,128]{1,0:T(8,128)S(1)} %bitcast.14), custom_call_target="tpu_custom_call" | custom-call | tf_op jit(solution)/shard_map/gather/pallas_call | solution.py:266
  55.5 19.2 %all_to_all.26 = f32[128,4,128]{2,1,0:T(4,128)S(1)} all-to-all(f32[128,4,128]{2,1,0:T(4,128)S(1)} %bitcast.15), channel_id=1, replica_groups=mesh['x'=4,'zh'=4,'z0'=2,'core'=2,'y'=4] {'z0','zh','x','y'}, dimensions={0} | all-to-all | bytes 524288 | tf_op jit(solution)/shard_map/all_to_all | solution.py:275
  74.6 0.1 zsum.1.mine
  74.7 3.3 %collective-permute-start.3 = (f32[128,128]{1,0:T(8,128)S(1)}, f32[128,128]{1,0:T(8,128)S(1)}, u32[]{:S(2)}, u32[]{:S(2)}) collective-permute-start(f32[128,128]{1,0:T(8,128)S(1)} %zsum.1.mine), channel_id=1, source_target_pairs={{0,4},{4,0},{1,5},{5,1},{2,6},{6,2},{3,7},{7,3},{8,12},{12,8},{9,1... | collective-permute-start | bytes 196616 | tf_op jit(solution)/shard_map/ppermute | solution.py:287
  78.1 0.9 collective-permute-done.3.other
  79.0 0.3 gram.1
  79.3 10.5 %all_to_all.27.refs_0_ = f32[16,8,256]{2,1,0:T(8,128)S(1)} all-to-all(f32[16,8,256]{2,1,0:T(8,128)S(1)} %bitcast.18), channel_id=1, replica_groups=mesh['x'=4,'zh'=4,'z0'=2,'core'=2,'y'=4] {'x','y'}, dimensions={0} | all-to-all | bytes 262144 | tf_op jit(solution)/shard_map/all_to_all | solution.py:307
  89.8 9.1 %all_to_all.28.refs_0_ = f32[8,8,256]{2,1,0:T(8,128)S(1)} all-to-all(f32[8,8,256]{2,1,0:T(8,128)S(1)} %sum_xy.1), channel_id=1, replica_groups=mesh['x'=4,'zh'=4,'z0'=2,'core'=2,'y'=4] {'z0','zh'}, dimensions={0} | all-to-all | bytes 131072 | tf_op jit(solution)/shard_map/all_to_all | solution.py:309
  99.0 15.1 %all_to_all.29 = f32[32,8,256]{2,1,0:T(8,128)S(1)} all-to-all(f32[32,8,256]{2,1,0:T(8,128)S(1)} %sum_z.1), channel_id=1, replica_groups=mesh['x'=4,'zh'=4,'z0'=2,'core'=2,'y'=4] {'core','x','y'}, dimensions={0} | all-to-all | bytes 524288 | tf_op jit(solution)/shard_map/all_to_all | solution.py:311
  114.1 6.7 %factor.1 = (f32[256,256]{1,0:T(8,128)}, f32[64,256]{1,0:T(8,128)}) custom-call(f32[256,256]{1,0:T(8,128)S(1)} %bitcast.16, f32[64,256]{1,0:T(8,128)S(1)} %get-tuple-element.11.rows_in), custom_call_target="tpu_custom_call" | custom-call | tf_op jit(solution)/shard_map/factor/pallas_call | solution.py:312
  (2 shorter events, 0.0 us)
Async XLA Ops:
  0.6 12.0 %copy-start.2 = (s32[64]{0:T(128)S(1)}, s32[64]{0:T(128)}, u32[]{:S(2)}) copy-start(s32[64]{0:T(128)} %param.5) | copy-start | bytes 772
  0.6 11.2 %collective-permute-start = (s32[64]{0:T(128)}, s32[64]{0:T(128)S(1)}, u32[]{:S(2)}, u32[]{:S(2)}) collective-permute-start(s32[64]{0:T(128)} %param.5), channel_id=1, source_target_pairs={{0,40},{8,32},{16,56},{24,48},{32,8},{40,0},{48,24},{56,16},{1,41}... | collective-permute-start | bytes 776 | tf_op jit(solution)/shard_map/ppermute | solution.py:244
  8.0 4.6 %collective-permute-start.2 = (s32[64]{0:T(128)}, s32[64]{0:T(128)S(1)}, u32[]{:S(2)}, u32[]{:S(2)}) collective-permute-start(s32[64]{0:T(128)} %param.5), channel_id=1, source_target_pairs={{0,48},{16,32},{32,16},{48,0},{1,49},{17,33},{33,17},{49,1},{2,50}... | collective-permute-start | bytes 776 | tf_op jit(solution)/shard_map/ppermute | solution.py:243
  8.3 4.4 %collective-permute-start.1 = (s32[64]{0:T(128)}, s32[64]{0:T(128)S(1)}, u32[]{:S(2)}, u32[]{:S(2)}) collective-permute-start(s32[64]{0:T(128)} %param.5), channel_id=1, source_target_pairs={{0,16},{16,0},{32,48},{48,32},{1,17},{17,1},{33,49},{49,33},{2,18}... | collective-permute-start | bytes 776 | tf_op jit(solution)/shard_map/ppermute | solution.py:243
  9.4 1.2 %copy-start = (bf16[2048,256]{1,0:T(8,128)(2,1)S(1)}, bf16[2048,256]{1,0:T(8,128)(2,1)}, u32[]{:S(2)}) copy-start(bf16[2048,256]{1,0:T(8,128)(2,1)} %matrix) | copy-start | bytes 3145732
  10.6 0.7 copy-start.1
  74.7 4.2 %collective-permute-start.3 = (f32[128,128]{1,0:T(8,128)S(1)}, f32[128,128]{1,0:T(8,128)S(1)}, u32[]{:S(2)}, u32[]{:S(2)}) collective-permute-start(f32[128,128]{1,0:T(8,128)S(1)} %zsum.1.mine), channel_id=1, source_target_pairs={{0,4},{4,0},{1,5},{5,1},{2,6},{6,2},{3,7},{7,3},{8,12},{12,8},{9,1... | collective-permute-start | bytes 196616 | tf_op jit(solution)/shard_map/ppermute | solution.py:287

commit v7 on v6

--- a/solution.py
+++ b/solution.py
@@ -172,9 +172,13 @@
         out[k] = value
 
 
-def factor_kernel(gram, rows_in, factor, rows_out, work):
+def factor_kernel(ids, mine, other, rows_in, factor, rows_out, work):
     rows_out[...] = rows_in[...]
-    work[...] = gram[...]
+    zero = jnp.broadcast_to(ids[1:2, :], (W // NC, LANES)) == 0
+    for t in range(W // LANES):
+        span = slice(t * LANES, (t + 1) * LANES)
+        work[: W // NC, span] = jnp.where(zero, mine[:, span], other[:, span])
+        work[W // NC :, span] = jnp.where(zero, other[:, span], mine[:, span])
     sub = lax.broadcasted_iota(jnp.int32, (8, LANES), 0)
     lane = lax.broadcasted_iota(jnp.int32, (8, LANES), 1)
     block = 64
@@ -307,17 +311,18 @@
     gram = lax.all_to_all(gram.reshape(NQ, 8, W), ("x", "y"), 0, 0, tiled=True)
     rows = spread(gram, NZ, 1.0, "sum_xy")
     rows = lax.all_to_all(rows, ("z0", "zh"), 0, 0, tiled=True)
-    rows = spread(rows, NC * NQ, 1.0 / (SAMP * 256), "sum_z")
-    gram = lax.all_to_all(rows, ("core", "x", "y"), 0, 0, tiled=True).reshape(W, W)
+    rows = spread(rows, NQ, 1.0 / (SAMP * 256), "sum_z")
+    mine = lax.all_to_all(rows, ("x", "y"), 0, 0, tiled=True).reshape(W // NC, W)
+    other = lax.ppermute(mine, "core", [(0, 1), (1, 0)])
     factor, sketch = pl.pallas_call(
         factor_kernel,
         out_shape=[shape(W, W), shape(SAMP, W)],
-        in_specs=[VMEM, VMEM],
+        in_specs=[VMEM] * 4,
         out_specs=[VMEM, VMEM],
         scratch_shapes=[pltpu.VMEM((W, W), F32)],
         compiler_params=params(4),
         name="factor",
-    )(gram, sketch)
+    )(ids, mine, other, sketch)
     return (sketch, factor)
 
 

time: 121 us -> 121 us (level)
  blocking collectives: 94.2 us -> 89.2 us
  starting transfers between devices: 11.9 us -> 15.9 us
    all_to_all x1, blocking collectives: 15.1 us -> 10.1 us  [on_device(): lax.all_to_all(rows, ('x', 'y'), 0, 0, tiled=True).reshape(W // NC, W)]
    ppermute x1 -> x2, starting transfers between devices: 3.35 us -> 7.35 us  [on_device(): other = lax.ppermute(mine, 'core', [(0, 1), (1, 0)])]
  transfers between devices with their start and end apart: 4 -> 5, of which waited for: 2 -> 3; matrix products, arithmetic and copies ran while one was open for 0% -> 0% of each run, Pallas kernels for 0% -> 0%
where the time goes in v7:
time: 121 us
  blocking collectives  89.2 us (74%)
  starting transfers between devices  15.9 us (13%)
  Pallas kernels  10.2 us (8%)
  waiting for transfers between devices  2.67 us (2%)
  local copies, waits for them, and re-layouts  2 us (2%)
    all_to_all x1, blocking collectives, on_device(): lax.all_to_all(packed, ('z0', 'core', 'x', 'y'), 0, 0, tiled=True)  40.2 us
    all_to_all x1, blocking collectives, on_device(): lax.all_to_all(sampled.reshape(CHIPS, COLS, LANES), ('z0', 'zh', 'x', 'y'...  19.2 us
    all_to_all x1, blocking collectives, on_device(): gram = lax.all_to_all(gram.reshape(NQ, 8, W), ('x', 'y'), 0, 0, tiled=True)  10.5 us
    all_to_all x1, blocking collectives, on_device(): lax.all_to_all(rows, ('x', 'y'), 0, 0, tiled=True).reshape(W // NC, W)  10.1 us
    all_to_all x1, blocking collectives, on_device(): rows = lax.all_to_all(rows, ('z0', 'zh'), 0, 0, tiled=True)  9.14 us
    ppermute x1, starting transfers between devices, on_device(): lax.ppermute(picks, ('zh', 'z0'), [(i, (i + 3 if i & 1 else i - 3) % NZ)...  7.38 us
    ppermute x2, starting transfers between devices, on_device(): other = lax.ppermute(mine, 'core', [(0, 1), (1, 0)])  7.35 us
    pallas_call x1, Pallas kernels, on_device(): pl.pallas_call(factor_kernel, out_shape=[shape(W, W), shape(SAMP, W)], in...  6.71 us
  transfers between devices with their start and end apart: 5, of which 3 were waited for; matrix products, arithmetic and copies ran while one was open for 0% of the time, Pallas kernels for 0%

profile of v7, /device:TPU:1, one launch (start us, length us, event | category | flops | bytes accessed | tf_op | source)
XLA Modules:
  0.0 120.8 jit_solution(3772992644027378919)
XLA Ops:
  0.6 0.0 copy-start.2
  0.6 7.4 %collective-permute-start = (s32[64]{0:T(128)}, s32[64]{0:T(128)S(1)}, u32[]{:S(2)}, u32[]{:S(2)}) collective-permute-start(s32[64]{0:T(128)} %param.5), channel_id=1, source_target_pairs={{0,40},{8,32},{16,56},{24,48},{32,8},{40,0},{48,24},{56,16},{1,41}... | collective-permute-start | bytes 776 | tf_op jit(solution)/shard_map/ppermute | solution.py:248
  8.0 0.3 collective-permute-start.2
  8.3 0.9 collective-permute-start.1
  9.2 0.1 pad_add_fusion
  9.3 0.1 broadcast_in_dim.2.ids.refs_0_
  9.4 0.0 copy-start
  9.4 1.2 %copy-done = bf16[2048,256]{1,0:T(8,128)(2,1)S(1)} copy-done((bf16[2048,256]{1,0:T(8,128)(2,1)S(1)}, bf16[2048,256]{1,0:T(8,128)(2,1)}, u32[]{:S(2)}) %copy-start) | copy-done | bytes 1048600
  10.6 0.0 copy-start.1
  10.6 0.7 copy-done.1
  11.3 0.6 local.1.table
  11.9 0.0 collective-permute-done
  11.9 0.8 collective-permute-done.2
  12.7 0.0 collective-permute-done.1
  12.7 0.0 copy-done.2
  12.7 0.2 pack.1
  12.8 40.2 %all_to_all.25 = f32[64,33,2,128]{3,2,1,0:T(2,128)S(1)} all-to-all(f32[64,33,2,128]{3,2,1,0:T(2,128)S(1)} %bitcast.13), channel_id=1, replica_groups=mesh['x'=4,'zh'=4,'z0'=2,'core'=2,'y'=4] {'z0','core','x','y'}, dimensions={0} | all-to-all | bytes 4325376 | tf_op jit(solution)/shard_map/all_to_all | solution.py:268
  53.1 2.4 %gather.1 = f32[2,4,64,128]{3,2,1,0:T(8,128)S(1)} custom-call(s32[2,128]{1,0:T(2,128)S(1)} %broadcast_in_dim.2.ids.refs_0_, f32[4224,128]{1,0:T(8,128)S(1)} %bitcast.14), custom_call_target="tpu_custom_call" | custom-call | tf_op jit(solution)/shard_map/gather/pallas_call | solution.py:270
  55.5 19.2 %all_to_all.26 = f32[128,4,128]{2,1,0:T(4,128)S(1)} all-to-all(f32[128,4,128]{2,1,0:T(4,128)S(1)} %bitcast.15), channel_id=1, replica_groups=mesh['x'=4,'zh'=4,'z0'=2,'core'=2,'y'=4] {'z0','zh','x','y'}, dimensions={0} | all-to-all | bytes 524288 | tf_op jit(solution)/shard_map/all_to_all | solution.py:279
  74.6 0.1 zsum.1.mine
  74.7 3.3 %collective-permute-start.3 = (f32[128,128]{1,0:T(8,128)S(1)}, f32[128,128]{1,0:T(8,128)S(1)}, u32[]{:S(2)}, u32[]{:S(2)}) collective-permute-start(f32[128,128]{1,0:T(8,128)S(1)} %zsum.1.mine), channel_id=1, source_target_pairs={{0,4},{4,0},{1,5},{5,1},{2,6},{6,2},{3,7},{7,3},{8,12},{12,8},{9,1... | collective-permute-start | bytes 196616 | tf_op jit(solution)/shard_map/ppermute | solution.py:291
  78.1 0.9 collective-permute-done.3.other
  79.0 0.3 gram.1
  79.3 10.5 %all_to_all.27.refs_0_ = f32[16,8,256]{2,1,0:T(8,128)S(1)} all-to-all(f32[16,8,256]{2,1,0:T(8,128)S(1)} %bitcast.19), channel_id=1, replica_groups=mesh['x'=4,'zh'=4,'z0'=2,'core'=2,'y'=4] {'x','y'}, dimensions={0} | all-to-all | bytes 262144 | tf_op jit(solution)/shard_map/all_to_all | solution.py:311
  89.8 9.1 %all_to_all.28.refs_0_ = f32[8,8,256]{2,1,0:T(8,128)S(1)} all-to-all(f32[8,8,256]{2,1,0:T(8,128)S(1)} %sum_xy.1), channel_id=1, replica_groups=mesh['x'=4,'zh'=4,'z0'=2,'core'=2,'y'=4] {'z0','zh'}, dimensions={0} | all-to-all | bytes 131072 | tf_op jit(solution)/shard_map/all_to_all | solution.py:313
  99.0 10.1 %all_to_all.29 = f32[16,8,256]{2,1,0:T(8,128)S(1)} all-to-all(f32[16,8,256]{2,1,0:T(8,128)S(1)} %sum_z.1), channel_id=1, replica_groups=mesh['x'=4,'zh'=4,'z0'=2,'core'=2,'y'=4] {'x','y'}, dimensions={0} | all-to-all | bytes 262144 | tf_op jit(solution)/shard_map/all_to_all | solution.py:315
  109.1 4.0 %collective-permute-start.4 = (f32[128,256]{1,0:T(8,128)S(1)}, f32[128,256]{1,0:T(8,128)S(1)}, u32[]{:S(2)}, u32[]{:S(2)}) collective-permute-start(f32[128,256]{1,0:T(8,128)S(1)} %bitcast.17), channel_id=1, source_target_pairs={{0,4},{4,0},{1,5},{5,1},{2,6},{6,2},{3,7},{7,3},{8,12},{12,8},{9,1... | collective-permute-start | bytes 393224 | tf_op jit(solution)/shard_map/ppermute | solution.py:316
  113.1 1.0 collective-permute-done.4.other
  114.1 6.7 %factor.1 = (f32[256,256]{1,0:T(8,128)}, f32[64,256]{1,0:T(8,128)}) custom-call(s32[2,128]{1,0:T(2,128)S(1)} %broadcast_in_dim.2.ids.refs_0_, f32[128,256]{1,0:T(8,128)S(1)} %bitcast.18, f32[128,256]{1,0:T(8,128)S(1)} %collective-permute-done.4.other, f32[64,256]{1,0:T(8,128)S(1)} %get-tuple-element.11.rows_in), custom_call_target="tpu_custom_call" | custom-call | tf_op jit(solution)/shard_map/factor/pallas_call | solution.py:317
  (2 shorter events, 0.0 us)
Async XLA Ops:
  0.6 12.0 %copy-start.2 = (s32[64]{0:T(128)S(1)}, s32[64]{0:T(128)}, u32[]{:S(2)}) copy-start(s32[64]{0:T(128)} %param.5) | copy-start | bytes 772
  0.6 11.2 %collective-permute-start = (s32[64]{0:T(128)}, s32[64]{0:T(128)S(1)}, u32[]{:S(2)}, u32[]{:S(2)}) collective-permute-start(s32[64]{0:T(128)} %param.5), channel_id=1, source_target_pairs={{0,40},{8,32},{16,56},{24,48},{32,8},{40,0},{48,24},{56,16},{1,41}... | collective-permute-start | bytes 776 | tf_op jit(solution)/shard_map/ppermute | solution.py:248
  8.0 4.6 %collective-permute-start.2 = (s32[64]{0:T(128)}, s32[64]{0:T(128)S(1)}, u32[]{:S(2)}, u32[]{:S(2)}) collective-permute-start(s32[64]{0:T(128)} %param.5), channel_id=1, source_target_pairs={{0,48},{16,32},{32,16},{48,0},{1,49},{17,33},{33,17},{49,1},{2,50}... | collective-permute-start | bytes 776 | tf_op jit(solution)/shard_map/ppermute | solution.py:247
  8.3 4.4 %collective-permute-start.1 = (s32[64]{0:T(128)}, s32[64]{0:T(128)S(1)}, u32[]{:S(2)}, u32[]{:S(2)}) collective-permute-start(s32[64]{0:T(128)} %param.5), channel_id=1, source_target_pairs={{0,16},{16,0},{32,48},{48,32},{1,17},{17,1},{33,49},{49,33},{2,18}... | collective-permute-start | bytes 776 | tf_op jit(solution)/shard_map/ppermute | solution.py:247
  9.4 1.2 %copy-start = (bf16[2048,256]{1,0:T(8,128)(2,1)S(1)}, bf16[2048,256]{1,0:T(8,128)(2,1)}, u32[]{:S(2)}) copy-start(bf16[2048,256]{1,0:T(8,128)(2,1)} %matrix) | copy-start | bytes 3145732
  10.6 0.7 copy-start.1
  74.7 4.2 %collective-permute-start.3 = (f32[128,128]{1,0:T(8,128)S(1)}, f32[128,128]{1,0:T(8,128)S(1)}, u32[]{:S(2)}, u32[]{:S(2)}) collective-permute-start(f32[128,128]{1,0:T(8,128)S(1)} %zsum.1.mine), channel_id=1, source_target_pairs={{0,4},{4,0},{1,5},{5,1},{2,6},{6,2},{3,7},{7,3},{8,12},{12,8},{9,1... | collective-permute-start | bytes 196616 | tf_op jit(solution)/shard_map/ppermute | solution.py:291
  109.1 5.0 %collective-permute-start.4 = (f32[128,256]{1,0:T(8,128)S(1)}, f32[128,256]{1,0:T(8,128)S(1)}, u32[]{:S(2)}, u32[]{:S(2)}) collective-permute-start(f32[128,256]{1,0:T(8,128)S(1)} %bitcast.17), channel_id=1, source_target_pairs={{0,4},{4,0},{1,5},{5,1},{2,6},{6,2},{3,7},{7,3},{8,12},{12,8},{9,1... | collective-permute-start | bytes 393224 | tf_op jit(solution)/shard_map/ppermute | solution.py:316

commit v8 on v7

--- a/solution.py
+++ b/solution.py
@@ -23,11 +23,16 @@
 LINE = (0, 2, 1, 3)
 F32 = jnp.float32
 HIGHEST = lax.Precision.HIGHEST
+HBM = pl.BlockSpec(memory_space=pltpu.HBM)
 VMEM = pl.BlockSpec(memory_space=pltpu.VMEM)
 
 
 def params(mib):
     return pltpu.CompilerParams(vmem_limit_bytes=mib * 1024 * 1024)
+
+
+def pinned(value):
+    return pltpu.with_memory_space_constraint(value, pltpu.HBM)
 
 
 def shape(*sizes):
@@ -56,7 +61,14 @@
     return parts[0]
 
 
-def local_kernel(matrix, signs, table):
+def local_kernel(matrix, signs, table, rows, marks, row_sems, mark_sem):
+    half = OUTER // 2
+    blocks = [pl.ds(o * ORDER, half * ORDER) for o in range(0, OUTER, half)]
+    fetches = [pltpu.make_async_copy(matrix.at[b], rows.at[b], row_sems.at[o]) for o, b in enumerate(blocks)]
+    mark = pltpu.make_async_copy(signs, marks, mark_sem)
+    mark.start()
+    for fetch in fetches:
+        fetch.start()
     row = lax.broadcasted_iota(jnp.int32, (ORDER, ORDER), 0)
     col = lax.broadcasted_iota(jnp.int32, (ORDER, ORDER), 1)
     both = row & col
@@ -64,9 +76,12 @@
     both = both ^ (both >> 2)
     both = both ^ (both >> 1)
     hadamard = (1 - 2 * (both & 1)).astype(F32).astype(jnp.bfloat16)
+    mark.wait()
     for o in range(OUTER):
-        block = matrix[o * ORDER : (o + 1) * ORDER, :].astype(F32)
-        sign = jnp.concatenate([signs[2 * o : 2 * o + 1, :], signs[2 * o + 1 : 2 * o + 2, :]], axis=1)
+        if o % half == 0:
+            fetches[o // half].wait()
+        block = rows[o * ORDER : (o + 1) * ORDER, :].astype(F32)
+        sign = jnp.concatenate([marks[2 * o : 2 * o + 1, :], marks[2 * o + 1 : 2 * o + 2, :]], axis=1)
         flipped = (block.T * sign.astype(F32)).astype(jnp.bfloat16)
         table[o] = jnp.dot(flipped, hadamard, preferred_element_type=F32)
 
@@ -251,11 +266,17 @@
     table = pl.pallas_call(
         local_kernel,
         out_shape=shape(OUTER, W, ORDER),
-        in_specs=[VMEM, VMEM],
+        in_specs=[HBM, HBM],
         out_specs=VMEM,
+        scratch_shapes=[
+            pltpu.VMEM((ROWS, W), jnp.bfloat16),
+            pltpu.VMEM((OUTER * 2, LANES), jnp.int32),
+            pltpu.SemaphoreType.DMA((2,)),
+            pltpu.SemaphoreType.DMA,
+        ],
         compiler_params=params(16),
         name="local",
-    )(matrix, signs.reshape(OUTER * 2, LANES))
+    )(pinned(matrix), pinned(signs.reshape(OUTER * 2, LANES)))
     packed = pl.pallas_call(
         pack_kernel,
         out_shape=shape(GROUP * CHUNK, LANES),

time: 121 us -> 121 us (level)
  local copies, waits for them, and re-layouts: 2 us -> 0.08 us
    unnamed x6 -> x2, local copies, waits for them, and re-layouts: 1.92 us -> 0.01 us
  transfers between devices with their start and end apart: 5 -> 5, of which waited for: 3 -> 3; matrix products, arithmetic and copies ran while one was open for 0% -> 0% of each run, Pallas kernels for 0% -> 1%
where the time goes in v8:
time: 121 us
  blocking collectives  89.2 us (74%)
  starting transfers between devices  15.9 us (13%)
  Pallas kernels  11.4 us (9%)
  waiting for transfers between devices  3.39 us (3%)
    all_to_all x1, blocking collectives, on_device(): lax.all_to_all(packed, ('z0', 'core', 'x', 'y'), 0, 0, tiled=True)  40.2 us
    all_to_all x1, blocking collectives, on_device(): lax.all_to_all(sampled.reshape(CHIPS, COLS, LANES), ('z0', 'zh', 'x', 'y'...  19.2 us
    all_to_all x1, blocking collectives, on_device(): gram = lax.all_to_all(gram.reshape(NQ, 8, W), ('x', 'y'), 0, 0, tiled=True)  10.5 us
    all_to_all x1, blocking collectives, on_device(): lax.all_to_all(rows, ('x', 'y'), 0, 0, tiled=True).reshape(W // NC, W)  10.1 us
    all_to_all x1, blocking collectives, on_device(): rows = lax.all_to_all(rows, ('z0', 'zh'), 0, 0, tiled=True)  9.14 us
    ppermute x1, starting transfers between devices, on_device(): lax.ppermute(picks, ('zh', 'z0'), [(i, (i + 3 if i & 1 else i - 3) % NZ)...  7.38 us
    ppermute x2, starting transfers between devices, on_device(): other = lax.ppermute(mine, 'core', [(0, 1), (1, 0)])  7.35 us
    pallas_call x1, Pallas kernels, on_device(): pl.pallas_call(factor_kernel, out_shape=[shape(W, W), shape(SAMP, W)], in...  6.71 us
  transfers between devices with their start and end apart: 5, of which 3 were waited for; matrix products, arithmetic and copies ran while one was open for 0% of the time, Pallas kernels for 1%

profile of v8, /device:TPU:1, one launch (start us, length us, event | category | flops | bytes accessed | tf_op | source)
XLA Modules:
  0.0 120.8 jit_solution(12059185330619647929)
XLA Ops:
  0.6 0.0 copy-start
  0.6 7.4 %collective-permute-start = (s32[64]{0:T(128)}, s32[64]{0:T(128)S(1)}, u32[]{:S(2)}, u32[]{:S(2)}) collective-permute-start(s32[64]{0:T(128)} %param.5), channel_id=1, source_target_pairs={{0,40},{8,32},{16,56},{24,48},{32,8},{40,0},{48,24},{56,16},{1,41}... | collective-permute-start | bytes 776 | tf_op jit(solution)/shard_map/ppermute | solution.py:263
  8.0 0.3 collective-permute-start.2
  8.3 0.9 collective-permute-start.1
  9.2 0.1 pad_add_fusion
  9.3 0.1 broadcast_in_dim.2.ids.refs_0_
  9.4 1.8 %local.1.table = f32[8,256,256]{2,1,0:T(8,128)S(1)} custom-call(bf16[2048,256]{1,0:T(8,128)(2,1)} %matrix, s32[16,128]{1,0:T(8,128)} %bitcast.24), custom_call_target="tpu_custom_call" | custom-call | tf_op jit(solution)/shard_map/local/pallas_call | solution.py:266
  11.1 0.0 collective-permute-done
  11.2 1.5 %collective-permute-done.2 = s32[64]{0:T(128)S(1)} collective-permute-done((s32[64]{0:T(128)}, s32[64]{0:T(128)S(1)}, u32[]{:S(2)}, u32[]{:S(2)}) %collective-permute-start.2) | collective-permute-done | bytes 288 | tf_op jit(solution)/shard_map/ppermute | solution.py:262
  12.7 0.0 collective-permute-done.1
  12.7 0.0 copy-done
  12.7 0.2 pack.1
  12.8 40.2 %all_to_all.25 = f32[64,33,2,128]{3,2,1,0:T(2,128)S(1)} all-to-all(f32[64,33,2,128]{3,2,1,0:T(2,128)S(1)} %bitcast.13), channel_id=1, replica_groups=mesh['x'=4,'zh'=4,'z0'=2,'core'=2,'y'=4] {'z0','core','x','y'}, dimensions={0} | all-to-all | bytes 4325376 | tf_op jit(solution)/shard_map/all_to_all | solution.py:289
  53.1 2.4 %gather.1 = f32[2,4,64,128]{3,2,1,0:T(8,128)S(1)} custom-call(s32[2,128]{1,0:T(2,128)S(1)} %broadcast_in_dim.2.ids.refs_0_, f32[4224,128]{1,0:T(8,128)S(1)} %bitcast.14), custom_call_target="tpu_custom_call" | custom-call | tf_op jit(solution)/shard_map/gather/pallas_call | solution.py:291
  55.5 19.2 %all_to_all.26 = f32[128,4,128]{2,1,0:T(4,128)S(1)} all-to-all(f32[128,4,128]{2,1,0:T(4,128)S(1)} %bitcast.15), channel_id=1, replica_groups=mesh['x'=4,'zh'=4,'z0'=2,'core'=2,'y'=4] {'z0','zh','x','y'}, dimensions={0} | all-to-all | bytes 524288 | tf_op jit(solution)/shard_map/all_to_all | solution.py:300
  74.6 0.1 zsum.1.mine
  74.7 3.3 %collective-permute-start.3 = (f32[128,128]{1,0:T(8,128)S(1)}, f32[128,128]{1,0:T(8,128)S(1)}, u32[]{:S(2)}, u32[]{:S(2)}) collective-permute-start(f32[128,128]{1,0:T(8,128)S(1)} %zsum.1.mine), channel_id=1, source_target_pairs={{0,4},{4,0},{1,5},{5,1},{2,6},{6,2},{3,7},{7,3},{8,12},{12,8},{9,1... | collective-permute-start | bytes 196616 | tf_op jit(solution)/shard_map/ppermute | solution.py:312
  78.1 0.9 collective-permute-done.3.other
  79.0 0.3 gram.1
  79.3 10.5 %all_to_all.27.refs_0_ = f32[16,8,256]{2,1,0:T(8,128)S(1)} all-to-all(f32[16,8,256]{2,1,0:T(8,128)S(1)} %bitcast.19), channel_id=1, replica_groups=mesh['x'=4,'zh'=4,'z0'=2,'core'=2,'y'=4] {'x','y'}, dimensions={0} | all-to-all | bytes 262144 | tf_op jit(solution)/shard_map/all_to_all | solution.py:332
  89.8 9.1 %all_to_all.28.refs_0_ = f32[8,8,256]{2,1,0:T(8,128)S(1)} all-to-all(f32[8,8,256]{2,1,0:T(8,128)S(1)} %sum_xy.1), channel_id=1, replica_groups=mesh['x'=4,'zh'=4,'z0'=2,'core'=2,'y'=4] {'z0','zh'}, dimensions={0} | all-to-all | bytes 131072 | tf_op jit(solution)/shard_map/all_to_all | solution.py:334
  99.0 10.1 %all_to_all.29 = f32[16,8,256]{2,1,0:T(8,128)S(1)} all-to-all(f32[16,8,256]{2,1,0:T(8,128)S(1)} %sum_z.1), channel_id=1, replica_groups=mesh['x'=4,'zh'=4,'z0'=2,'core'=2,'y'=4] {'x','y'}, dimensions={0} | all-to-all | bytes 262144 | tf_op jit(solution)/shard_map/all_to_all | solution.py:336
  109.1 4.0 %collective-permute-start.4 = (f32[128,256]{1,0:T(8,128)S(1)}, f32[128,256]{1,0:T(8,128)S(1)}, u32[]{:S(2)}, u32[]{:S(2)}) collective-permute-start(f32[128,256]{1,0:T(8,128)S(1)} %bitcast.17), channel_id=1, source_target_pairs={{0,4},{4,0},{1,5},{5,1},{2,6},{6,2},{3,7},{7,3},{8,12},{12,8},{9,1... | collective-permute-start | bytes 393224 | tf_op jit(solution)/shard_map/ppermute | solution.py:337
  113.1 1.0 collective-permute-done.4.other
  114.1 6.7 %factor.1 = (f32[256,256]{1,0:T(8,128)}, f32[64,256]{1,0:T(8,128)}) custom-call(s32[2,128]{1,0:T(2,128)S(1)} %broadcast_in_dim.2.ids.refs_0_, f32[128,256]{1,0:T(8,128)S(1)} %bitcast.18, f32[128,256]{1,0:T(8,128)S(1)} %collective-permute-done.4.other, f32[64,256]{1,0:T(8,128)S(1)} %get-tuple-element.11.rows_in), custom_call_target="tpu_custom_call" | custom-call | tf_op jit(solution)/shard_map/factor/pallas_call | solution.py:338
  (2 shorter events, 0.0 us)
Async XLA Ops:
  0.6 12.0 %copy-start = (s32[64]{0:T(128)S(1)}, s32[64]{0:T(128)}, u32[]{:S(2)}) copy-start(s32[64]{0:T(128)} %param.5) | copy-start | bytes 772
  0.6 10.5 %collective-permute-start = (s32[64]{0:T(128)}, s32[64]{0:T(128)S(1)}, u32[]{:S(2)}, u32[]{:S(2)}) collective-permute-start(s32[64]{0:T(128)} %param.5), channel_id=1, source_target_pairs={{0,40},{8,32},{16,56},{24,48},{32,8},{40,0},{48,24},{56,16},{1,41}... | collective-permute-start | bytes 776 | tf_op jit(solution)/shard_map/ppermute | solution.py:263
  8.0 4.6 %collective-permute-start.2 = (s32[64]{0:T(128)}, s32[64]{0:T(128)S(1)}, u32[]{:S(2)}, u32[]{:S(2)}) collective-permute-start(s32[64]{0:T(128)} %param.5), channel_id=1, source_target_pairs={{0,48},{16,32},{32,16},{48,0},{1,49},{17,33},{33,17},{49,1},{2,50}... | collective-permute-start | bytes 776 | tf_op jit(solution)/shard_map/ppermute | solution.py:262
  8.3 4.4 %collective-permute-start.1 = (s32[64]{0:T(128)}, s32[64]{0:T(128)S(1)}, u32[]{:S(2)}, u32[]{:S(2)}) collective-permute-start(s32[64]{0:T(128)} %param.5), channel_id=1, source_target_pairs={{0,16},{16,0},{32,48},{48,32},{1,17},{17,1},{33,49},{49,33},{2,18}... | collective-permute-start | bytes 776 | tf_op jit(solution)/shard_map/ppermute | solution.py:262
  74.7 4.2 %collective-permute-start.3 = (f32[128,128]{1,0:T(8,128)S(1)}, f32[128,128]{1,0:T(8,128)S(1)}, u32[]{:S(2)}, u32[]{:S(2)}) collective-permute-start(f32[128,128]{1,0:T(8,128)S(1)} %zsum.1.mine), channel_id=1, source_target_pairs={{0,4},{4,0},{1,5},{5,1},{2,6},{6,2},{3,7},{7,3},{8,12},{12,8},{9,1... | collective-permute-start | bytes 196616 | tf_op jit(solution)/shard_map/ppermute | solution.py:312
  109.1 5.0 %collective-permute-start.4 = (f32[128,256]{1,0:T(8,128)S(1)}, f32[128,256]{1,0:T(8,128)S(1)}, u32[]{:S(2)}, u32[]{:S(2)}) collective-permute-start(f32[128,256]{1,0:T(8,128)S(1)} %bitcast.17), channel_id=1, source_target_pairs={{0,4},{4,0},{1,5},{5,1},{2,6},{6,2},{3,7},{7,3},{8,12},{12,8},{9,1... | collective-permute-start | bytes 393224 | tf_op jit(solution)/shard_map/ppermute | solution.py:337

commit v9 on v8

--- a/solution.py
+++ b/solution.py
@@ -20,7 +20,7 @@
 CHUNK = OUTER * 8 + 2
 CHIPS = NZH * NZ0 * NX * NY
 LANES = 128
-LINE = (0, 2, 1, 3)
+LINE = (0, 2, 3, 1)
 F32 = jnp.float32
 HIGHEST = lax.Precision.HIGHEST
 HBM = pl.BlockSpec(memory_space=pltpu.HBM)

time: 121 us -> 120 us (level)
  blocking collectives: 89.2 us -> 87.1 us
    all_to_all x1, blocking collectives: 19.2 us -> 16.8 us  [on_device(): lax.all_to_all(sampled.reshape(CHIPS, COLS, LANES), ('z0', 'zh', 'x', 'y'...]
  transfers between devices with their start and end apart: 5 -> 5, of which waited for: 3 -> 4; matrix products, arithmetic and copies ran while one was open for 0% -> 0% of each run, Pallas kernels for 1% -> 1%
where the time goes in v9:
time: 120 us
  blocking collectives  87.1 us (73%)
  starting transfers between devices  15.9 us (13%)
  Pallas kernels  11.5 us (10%)
  waiting for transfers between devices  4.57 us (4%)
    all_to_all x1, blocking collectives, on_device(): lax.all_to_all(packed, ('z0', 'core', 'x', 'y'), 0, 0, tiled=True)  40.5 us
    all_to_all x1, blocking collectives, on_device(): lax.all_to_all(sampled.reshape(CHIPS, COLS, LANES), ('z0', 'zh', 'x', 'y'...  16.8 us
    all_to_all x1, blocking collectives, on_device(): gram = lax.all_to_all(gram.reshape(NQ, 8, W), ('x', 'y'), 0, 0, tiled=True)  10.5 us
    all_to_all x1, blocking collectives, on_device(): lax.all_to_all(rows, ('x', 'y'), 0, 0, tiled=True).reshape(W // NC, W)  10.1 us
    all_to_all x1, blocking collectives, on_device(): rows = lax.all_to_all(rows, ('z0', 'zh'), 0, 0, tiled=True)  9.14 us
    ppermute x1, starting transfers between devices, on_device(): lax.ppermute(picks, ('zh', 'z0'), [(i, (i + 3 if i & 1 else i - 3) % NZ)...  7.38 us
    ppermute x2, starting transfers between devices, on_device(): other = lax.ppermute(mine, 'core', [(0, 1), (1, 0)])  7.36 us
    pallas_call x1, Pallas kernels, on_device(): pl.pallas_call(factor_kernel, out_shape=[shape(W, W), shape(SAMP, W)], in...  6.71 us
  transfers between devices with their start and end apart: 5, of which 4 were waited for; matrix products, arithmetic and copies ran while one was open for 0% of the time, Pallas kernels for 1%

profile of v9, /device:TPU:1, one launch (start us, length us, event | category | flops | bytes accessed | tf_op | source)
XLA Modules:
  0.0 119.9 jit_solution(8527757996418104910)
XLA Ops:
  0.6 0.0 copy-start
  0.6 7.4 %collective-permute-start = (s32[64]{0:T(128)}, s32[64]{0:T(128)S(1)}, u32[]{:S(2)}, u32[]{:S(2)}) collective-permute-start(s32[64]{0:T(128)} %param.5), channel_id=1, source_target_pairs={{0,40},{8,32},{16,56},{24,48},{32,8},{40,0},{48,24},{56,16},{1,41}... | collective-permute-start | bytes 776 | tf_op jit(solution)/shard_map/ppermute | solution.py:263
  8.0 1.2 collective-permute-start.2
  9.2 0.0 collective-permute-start.1
  9.2 0.1 pad_add_fusion
  9.3 0.1 broadcast_in_dim.2.ids.refs_0_
  9.4 1.8 %local.1.table = f32[8,256,256]{2,1,0:T(8,128)S(1)} custom-call(bf16[2048,256]{1,0:T(8,128)(2,1)} %matrix, s32[16,128]{1,0:T(8,128)} %bitcast.24), custom_call_target="tpu_custom_call" | custom-call | tf_op jit(solution)/shard_map/local/pallas_call | solution.py:266
  11.2 0.0 collective-permute-done
  11.2 0.3 collective-permute-done.2
  11.4 2.4 %collective-permute-done.1 = s32[64]{0:T(128)S(1)} collective-permute-done((s32[64]{0:T(128)}, s32[64]{0:T(128)S(1)}, u32[]{:S(2)}, u32[]{:S(2)}) %collective-permute-start.1) | collective-permute-done | bytes 288 | tf_op jit(solution)/shard_map/ppermute | solution.py:262
  13.8 0.0 copy-done
  13.9 0.2 pack.1
  14.0 40.5 %all_to_all.25 = f32[64,33,2,128]{3,2,1,0:T(2,128)S(1)} all-to-all(f32[64,33,2,128]{3,2,1,0:T(2,128)S(1)} %bitcast.13), channel_id=1, replica_groups=mesh['x'=4,'zh'=4,'z0'=2,'core'=2,'y'=4] {'z0','core','x','y'}, dimensions={0} | all-to-all | bytes 4325376 | tf_op jit(solution)/shard_map/all_to_all | solution.py:289
  54.5 2.4 %gather.1 = f32[2,4,64,128]{3,2,1,0:T(8,128)S(1)} custom-call(s32[2,128]{1,0:T(2,128)S(1)} %broadcast_in_dim.2.ids.refs_0_, f32[4224,128]{1,0:T(8,128)S(1)} %bitcast.14), custom_call_target="tpu_custom_call" | custom-call | tf_op jit(solution)/shard_map/gather/pallas_call | solution.py:291
  56.9 16.8 %all_to_all.26 = f32[128,4,128]{2,1,0:T(4,128)S(1)} all-to-all(f32[128,4,128]{2,1,0:T(4,128)S(1)} %bitcast.15), channel_id=1, replica_groups=mesh['x'=4,'zh'=4,'z0'=2,'core'=2,'y'=4] {'z0','zh','x','y'}, dimensions={0} | all-to-all | bytes 524288 | tf_op jit(solution)/shard_map/all_to_all | solution.py:300
  73.7 0.1 zsum.1.mine
  73.8 3.3 %collective-permute-start.3 = (f32[128,128]{1,0:T(8,128)S(1)}, f32[128,128]{1,0:T(8,128)S(1)}, u32[]{:S(2)}, u32[]{:S(2)}) collective-permute-start(f32[128,128]{1,0:T(8,128)S(1)} %zsum.1.mine), channel_id=1, source_target_pairs={{0,4},{4,0},{1,5},{5,1},{2,6},{6,2},{3,7},{7,3},{8,12},{12,8},{9,1... | collective-permute-start | bytes 196616 | tf_op jit(solution)/shard_map/ppermute | solution.py:312
  77.2 0.9 collective-permute-done.3.other
  78.1 0.3 gram.1
  78.4 10.5 %all_to_all.27.refs_0_ = f32[16,8,256]{2,1,0:T(8,128)S(1)} all-to-all(f32[16,8,256]{2,1,0:T(8,128)S(1)} %bitcast.19), channel_id=1, replica_groups=mesh['x'=4,'zh'=4,'z0'=2,'core'=2,'y'=4] {'x','y'}, dimensions={0} | all-to-all | bytes 262144 | tf_op jit(solution)/shard_map/all_to_all | solution.py:332
  88.9 9.1 %all_to_all.28.refs_0_ = f32[8,8,256]{2,1,0:T(8,128)S(1)} all-to-all(f32[8,8,256]{2,1,0:T(8,128)S(1)} %sum_xy.1), channel_id=1, replica_groups=mesh['x'=4,'zh'=4,'z0'=2,'core'=2,'y'=4] {'z0','zh'}, dimensions={0} | all-to-all | bytes 131072 | tf_op jit(solution)/shard_map/all_to_all | solution.py:334
  98.1 10.1 %all_to_all.29 = f32[16,8,256]{2,1,0:T(8,128)S(1)} all-to-all(f32[16,8,256]{2,1,0:T(8,128)S(1)} %sum_z.1), channel_id=1, replica_groups=mesh['x'=4,'zh'=4,'z0'=2,'core'=2,'y'=4] {'x','y'}, dimensions={0} | all-to-all | bytes 262144 | tf_op jit(solution)/shard_map/all_to_all | solution.py:336
  108.2 4.0 %collective-permute-start.4 = (f32[128,256]{1,0:T(8,128)S(1)}, f32[128,256]{1,0:T(8,128)S(1)}, u32[]{:S(2)}, u32[]{:S(2)}) collective-permute-start(f32[128,256]{1,0:T(8,128)S(1)} %bitcast.17), channel_id=1, source_target_pairs={{0,4},{4,0},{1,5},{5,1},{2,6},{6,2},{3,7},{7,3},{8,12},{12,8},{9,1... | collective-permute-start | bytes 393224 | tf_op jit(solution)/shard_map/ppermute | solution.py:337
  112.2 1.0 collective-permute-done.4.other
  113.2 6.7 %factor.1 = (f32[256,256]{1,0:T(8,128)}, f32[64,256]{1,0:T(8,128)}) custom-call(s32[2,128]{1,0:T(2,128)S(1)} %broadcast_in_dim.2.ids.refs_0_, f32[128,256]{1,0:T(8,128)S(1)} %bitcast.18, f32[128,256]{1,0:T(8,128)S(1)} %collective-permute-done.4.other, f32[64,256]{1,0:T(8,128)S(1)} %get-tuple-element.11.rows_in), custom_call_target="tpu_custom_call" | custom-call | tf_op jit(solution)/shard_map/factor/pallas_call | solution.py:338
  (2 shorter events, 0.0 us)
Async XLA Ops:
  0.6 13.2 %copy-start = (s32[64]{0:T(128)S(1)}, s32[64]{0:T(128)}, u32[]{:S(2)}) copy-start(s32[64]{0:T(128)} %param.5) | copy-start | bytes 772
  0.6 10.5 %collective-permute-start = (s32[64]{0:T(128)}, s32[64]{0:T(128)S(1)}, u32[]{:S(2)}, u32[]{:S(2)}) collective-permute-start(s32[64]{0:T(128)} %param.5), channel_id=1, source_target_pairs={{0,40},{8,32},{16,56},{24,48},{32,8},{40,0},{48,24},{56,16},{1,41}... | collective-permute-start | bytes 776 | tf_op jit(solution)/shard_map/ppermute | solution.py:263
  8.0 3.4 %collective-permute-start.2 = (s32[64]{0:T(128)}, s32[64]{0:T(128)S(1)}, u32[]{:S(2)}, u32[]{:S(2)}) collective-permute-start(s32[64]{0:T(128)} %param.5), channel_id=1, source_target_pairs={{0,16},{16,0},{32,48},{48,32},{1,17},{17,1},{33,49},{49,33},{2,18}... | collective-permute-start | bytes 776 | tf_op jit(solution)/shard_map/ppermute | solution.py:262
  9.2 4.6 %collective-permute-start.1 = (s32[64]{0:T(128)}, s32[64]{0:T(128)S(1)}, u32[]{:S(2)}, u32[]{:S(2)}) collective-permute-start(s32[64]{0:T(128)} %param.5), channel_id=1, source_target_pairs={{0,48},{16,32},{32,16},{48,0},{1,49},{17,33},{33,17},{49,1},{2,50}... | collective-permute-start | bytes 776 | tf_op jit(solution)/shard_map/ppermute | solution.py:262
  73.8 4.2 %collective-permute-start.3 = (f32[128,128]{1,0:T(8,128)S(1)}, f32[128,128]{1,0:T(8,128)S(1)}, u32[]{:S(2)}, u32[]{:S(2)}) collective-permute-start(f32[128,128]{1,0:T(8,128)S(1)} %zsum.1.mine), channel_id=1, source_target_pairs={{0,4},{4,0},{1,5},{5,1},{2,6},{6,2},{3,7},{7,3},{8,12},{12,8},{9,1... | collective-permute-start | bytes 196616 | tf_op jit(solution)/shard_map/ppermute | solution.py:312
  108.2 5.0 %collective-permute-start.4 = (f32[128,256]{1,0:T(8,128)S(1)}, f32[128,256]{1,0:T(8,128)S(1)}, u32[]{:S(2)}, u32[]{:S(2)}) collective-permute-start(f32[128,256]{1,0:T(8,128)S(1)} %bitcast.17), channel_id=1, source_target_pairs={{0,4},{4,0},{1,5},{5,1},{2,6},{6,2},{3,7},{7,3},{8,12},{12,8},{9,1... | collective-permute-start | bytes 393224 | tf_op jit(solution)/shard_map/ppermute | solution.py:337
